TPU v7x, 128 devices: a whole 4x4x4 slice. The times are simulated.
128 devices in a mesh: grp: 8 (over x_lo, y), tile: 16 (over x_hi, z, core).
Axes of the slice: x: 4 (x_hi: 2, x_lo: 2; x = x_hi * 2 + x_lo), y: 4, z: 4, core: 2. Of those that a mesh axis runs over, the one named last changes fastest.
Arguments:
- pressure: float32 [2, 32, 384, 768], P(None, None, ('grp', 'tile')), may hold values from -6 to 6
- u_wind: float32 [2, 32, 384, 768], P(None, None, ('grp', 'tile')), may hold values from -4 to 4
- v_wind: float32 [2, 32, 384, 768], P(None, None, ('grp', 'tile')), may hold values from -4 to 4
- stiffness: float32 [2, 32, 384, 768], P(None, None, ('grp', 'tile')), may hold values from 0.5 to 2
- vertical: float32 [32, 32], replicated, may hold values from -1 to 1
- nest_row0: int32 [60], replicated, may hold values from 1 to 60, as said below
- nest_col0: int32 [511], replicated, may hold values from 1 to 511, as said below
Outputs:
- pressure_out: float32 [2, 32, 384, 768], P(None, None, ('grp', 'tile'))
- u_out: float32 [2, 32, 384, 768], P(None, None, ('grp', 'tile'))
- v_out: float32 [2, 32, 384, 768], P(None, None, ('grp', 'tile'))
Inputs may be any that keep to these rules, and one draw needn't show every extreme that they name: `nest_row0`: each whole number of the range appears exactly once. `nest_col0`: each whole number of the range appears exactly once.
All inputs are finite; a program needn't handle non-finite values.
Results may differ from a plain program's by a relative error of at most 0.0001.
Values sent between devices are 32-bit elements; how exact they have to be, the bound alone decides.
A program may use at most 64 MiB of HBM per device.

v0:
```python
import jax
import jax.numpy as jnp
from jax import lax
from jax.sharding import PartitionSpec as P

RATIO = 3
OUTER = 2


COURANT = 0.3
MIXING = 0.15


def passed_along(value, axis, steps):
    count = lax.axis_size(axis)
    initial, last = (max(0, -steps), min(count, count - steps))
    return lax.ppermute(value, axis, [(source, source + steps) for source in range(initial, last)])


def mixlevels(vertical, field):
    return field + MIXING * jnp.einsum(
        "ab,bxy->axy", vertical, field, precision=lax.Precision.HIGHEST
    )


def per_device(pressure, u_wind, v_wind, stiffness, vertical, nest_row0, nest_col0):
    levels, rows, cols = (pressure.shape[1], pressure.shape[2], pressure.shape[3])
    tiles = lax.axis_size("tile")
    total = lax.axis_size("grp") * tiles
    device = lax.axis_index("grp") * tiles + lax.axis_index("tile")
    part = rows // RATIO
    win_x = total * part
    win_y = cols // RATIO
    row0 = nest_row0[0]
    col0 = nest_col0[0]
    zero = jnp.zeros((), jnp.int32)
    owned_global = device * rows + jnp.arange(rows, dtype=jnp.int32)
    window_rows = row0 + jnp.arange(win_x, dtype=jnp.int32)
    selector = (window_rows[:, None] == owned_global[None, :]).astype(jnp.float32)
    owned_rows = jnp.sum(selector, axis=0) > 0.5
    col_index = jnp.arange(cols, dtype=jnp.int32)
    col_mask = (col_index >= col0) & (col_index < col0 + win_y)
    last_row = (jnp.arange(rows) == rows - 1)[None, :, None]
    first_dev = device == 0
    last_dev = device == total - 1
    zero_edge = jnp.zeros((levels, 1, cols), jnp.float32)

    def take_row(field, target):
        local = target - device * rows
        inside = (local >= 0) & (local < rows)
        picked = lax.dynamic_slice_in_dim(field, jnp.clip(local, 0, rows - 1), 1, 1)[:, 0, :]
        picked = lax.dynamic_slice_in_dim(picked, col0, win_y, 1)
        return picked * inside.astype(jnp.float32)

    def take_col(field, target):
        picked = lax.dynamic_slice_in_dim(field, target, 1, 2)[:, :, 0]
        return jnp.einsum("ri,li->lr", selector, picked, precision=lax.Precision.HIGHEST)

    def substep(
        p_field, u_field, v_field, k_field, top_edge, bottom_edge, right_col, left_col, periodic
    ):
        from_above = passed_along(p_field[:, :1, :], ("grp", "tile"), -1)
        above = jnp.where(last_dev, top_edge, from_above)
        p_up = jnp.concatenate([p_field[:, 1:], above], axis=1)
        u_new = u_field - COURANT * (p_up - p_field)
        right = p_field[:, :, :1] if periodic else right_col
        p_rt = jnp.concatenate([p_field[:, :, 1:], right], axis=2)
        v_new = v_field - COURANT * (p_rt - p_field)
        if periodic:
            u_new = jnp.where(last_dev & last_row, 0.0, u_new)
        from_below = passed_along(u_new[:, -1:, :], ("grp", "tile"), 1)
        below = jnp.where(first_dev, bottom_edge, from_below)
        left = v_new[:, :, -1:] if periodic else left_col
        u_dn = jnp.concatenate([below, u_new[:, :-1]], axis=1)
        v_dn = jnp.concatenate([left, v_new[:, :, :-1]], axis=2)
        q_field = p_field - COURANT * k_field * (u_new - u_dn + (v_new - v_dn))
        return (mixlevels(vertical, q_field), u_new, v_new)

    par_p, nst_p = (pressure[0], pressure[1])
    par_u, nst_u = (u_wind[0], u_wind[1])
    par_v, nst_v = (v_wind[0], v_wind[1])
    par_k, nst_k = (stiffness[0], stiffness[1])
    for outer in range(OUTER):
        row_p = take_row(par_p, row0 + win_x)
        row_u = take_row(par_u, row0 - 1)
        col_p = take_col(par_p, col0 + win_y)
        col_v = take_col(par_v, col0 - 1)
        row_p, row_u, col_p, col_v = lax.psum((row_p, row_u, col_p, col_v), ("grp", "tile"))
        above_n = jnp.repeat(row_p, RATIO, axis=1)[:, None, :]
        below_n = jnp.repeat(row_u, RATIO, axis=1)[:, None, :]
        right_n = jnp.repeat(
            lax.dynamic_slice_in_dim(col_p, device * part, part, 1), RATIO, axis=1
        )[:, :, None]
        left_n = jnp.repeat(lax.dynamic_slice_in_dim(col_v, device * part, part, 1), RATIO, axis=1)[
            :, :, None
        ]
        par_p, par_u, par_v = substep(
            par_p, par_u, par_v, par_k, zero_edge, zero_edge, None, None, True
        )
        for inner in range(RATIO):
            nst_p, nst_u, nst_v = substep(
                nst_p, nst_u, nst_v, nst_k, above_n, below_n, right_n, left_n, False
            )
        averaged = nst_p.reshape(levels, part, RATIO, win_y, RATIO).mean(axis=(2, 4))
        window = jnp.zeros((levels, win_x, win_y), jnp.float32)
        window = lax.dynamic_update_slice(window, averaged, (zero, device * part, zero))
        window = lax.psum(window, ("grp", "tile"))
        local = jnp.einsum("ri,lrc->lic", selector, window, precision=lax.Precision.HIGHEST)
        placed = lax.dynamic_update_slice(
            jnp.zeros((levels, rows, cols), jnp.float32), local, (zero, zero, col0)
        )
        replace = owned_rows[None, :, None] & col_mask[None, None, :]
        par_p = jnp.where(replace, placed, par_p)
    return (jnp.stack([par_p, nst_p]), jnp.stack([par_u, nst_u]), jnp.stack([par_v, nst_v]))


def solution(mesh):
    return jax.shard_map(
        per_device,
        mesh=mesh,
        in_specs=(
            P(None, None, ("grp", "tile"), None),
            P(None, None, ("grp", "tile"), None),
            P(None, None, ("grp", "tile"), None),
            P(None, None, ("grp", "tile"), None),
            P(),
            P(),
            P(),
        ),
        out_specs=(
            P(None, None, ("grp", "tile"), None),
            P(None, None, ("grp", "tile"), None),
            P(None, None, ("grp", "tile"), None),
        ),
        check_vma=False,
    )
```

profile of v0, /device:TPU:8, one launch (start us, length us, event | category | flops | bytes accessed | tf_op | source)
XLA Modules:
  0.0 747.3 jit_solution(98349768698511326)
XLA Ops:
  8.4 7.7 %collective-permute-start = (f32[32,1,768]{2,0,1:T(8,128)S(1)}, f32[32,1,768]{2,0,1:T(8,128)}, u32[]{:S(2)}, u32[]{:S(2)}) collective-permute-start(f32[32,1,768]{2,0,1:T(8,128)S(1)} %slice.249), channel_id=1, source_target_pairs={{1,0},{2,1},{3,2},{4,3},{5,4},{6,5},{7,6},{8,7},{9,8},{10,9},{11,1... | collective-permute-start | bytes 294920 | tf_op jit(solution)/shard_map/ppermute | solution.py:17
  16.8 2.6 collective-permute-start.6
  33.1 140.5 %all-reduce.13.cloned.1.call-done = (f32[32,128]{0,1:T(8,128)}, f32[32,128]{0,1:T(8,128)}, f32[32,256]{1,0:T(8,128)}, f32[32,256]{1,0:T(8,128)}) async-done(((f32[32,128]{0,1:T(8,128)}, f32[32,128]{0,1:T(8,128)}, f32[32,256]{1,0:T(8,128)}, f32[32,256]{1,0:T(8,128)}), (f32[32,128]{0,1:T(8,128)}, f32[32,128]{0,1:T(8,128)}, f32[32,256]{1,0:T(8,128)}, f32[32,256]{1,0:T(8,128)})) %all-reduce.13.cloned.1.call-update) | async-done | bytes 98320 | tf_op jit(solution)/shard_map/psum | solution.py:88
  180.3 1.9 collective-permute-start.1
  182.9 7.8 %collective-permute-done.1 = f32[32,1,768]{2,0,1:T(8,128)S(1)} collective-permute-done((f32[32,1,768]{2,0,1:T(8,128)S(1)}, f32[32,1,768]{2,0,1:T(8,128)S(1)}, u32[]{:S(2)}, u32[]{:S(2)}) %collective-permute-start.1) | collective-permute-done | bytes 98336 | tf_op jit(solution)/shard_map/ppermute | solution.py:17
  191.5 1.9 collective-permute-start.2
  193.5 2.0 collective-permute-done.2
  195.7 1.9 collective-permute-start.3
  197.7 8.6 %collective-permute-done.3 = f32[32,1,768]{2,0,1:T(8,128)S(1)} collective-permute-done((f32[32,1,768]{2,0,1:T(8,128)S(1)}, f32[32,1,768]{2,0,1:T(8,128)S(1)}, u32[]{:S(2)}, u32[]{:S(2)}) %collective-permute-start.3) | collective-permute-done | bytes 98336 | tf_op jit(solution)/shard_map/ppermute | solution.py:17
  206.9 1.9 collective-permute-start.4
  209.0 2.0 collective-permute-done.4
  211.2 1.9 collective-permute-start.5
  213.1 8.6 %collective-permute-done.5 = f32[32,1,768]{2,0,1:T(8,128)S(1)} collective-permute-done((f32[32,1,768]{2,0,1:T(8,128)S(1)}, f32[32,1,768]{2,0,1:T(8,128)S(1)}, u32[]{:S(2)}, u32[]{:S(2)}) %collective-permute-start.5) | collective-permute-done | bytes 98336 | tf_op jit(solution)/shard_map/ppermute | solution.py:17
  224.8 2.5 broadcast.123.clone
  230.7 1.9 collective-permute-start.7
  235.0 6.2 collective-permute-done.7
  241.3 138.4 %all-reduce.7.cloned.1.call-done = f32[32,128,256]{2,1,0:T(8,128)} async-done(((f32[32,128,256]{2,1,0:T(8,128)}), f32[32,128,256]{2,1,0:T(8,128)}) %all-reduce.7.cloned.1.call-update) | async-done | bytes 4194320 | tf_op jit(solution)/shard_map/psum | solution.py:107
  379.7 3.6 fusion.181
  390.3 4.7 collective-permute-start.8
  395.0 135.5 %all-reduce.11.cloned.1.call-done = (f32[32,128]{0,1:T(8,128)}, f32[32,128]{0,1:T(8,128)}, f32[32,256]{1,0:T(8,128)}, f32[32,256]{1,0:T(8,128)}) async-done(((f32[32,128]{0,1:T(8,128)}, f32[32,128]{0,1:T(8,128)}, f32[32,256]{1,0:T(8,128)}, f32[32,256]{1,0:T(8,128)}), (f32[32,128]{0,1:T(8,128)}, f32[32,128]{0,1:T(8,128)}, f32[32,256]{1,0:T(8,128)}, f32[32,256]{1,0:T(8,128)})) %all-reduce.11.cloned.1.call-update) | async-done | bytes 98320 | tf_op jit(solution)/shard_map/psum | solution.py:88
  539.2 8.0 %collective-permute-done.9 = f32[32,1,768]{2,0,1:T(8,128)S(1)} collective-permute-done((f32[32,1,768]{2,0,1:T(8,128)}, f32[32,1,768]{2,0,1:T(8,128)S(1)}, u32[]{:S(2)}, u32[]{:S(2)}) %collective-permute-start.9) | collective-permute-done | bytes 98336 | tf_op jit(solution)/shard_map/ppermute | solution.py:17
  550.0 2.0 collective-permute-done.10
  552.2 2.1 collective-permute-start.11
  554.3 8.4 %collective-permute-done.11 = f32[32,1,768]{2,0,1:T(8,128)S(1)} collective-permute-done((f32[32,1,768]{2,0,1:T(8,128)S(1)}, f32[32,1,768]{2,0,1:T(8,128)S(1)}, u32[]{:S(2)}, u32[]{:S(2)}) %collective-permute-start.11) | collective-permute-done | bytes 98336 | tf_op jit(solution)/shard_map/ppermute | solution.py:17
  563.4 1.9 collective-permute-start.12
  565.5 2.0 collective-permute-done.12
  569.6 8.6 %collective-permute-done.13 = f32[32,1,768]{2,0,1:T(8,128)S(1)} collective-permute-done((f32[32,1,768]{2,0,1:T(8,128)S(1)}, f32[32,1,768]{2,0,1:T(8,128)S(1)}, u32[]{:S(2)}, u32[]{:S(2)}) %collective-permute-start.13) | collective-permute-done | bytes 98336 | tf_op jit(solution)/shard_map/ppermute | solution.py:17
  579.6 2.5 broadcast.123
  586.0 2.0 collective-permute-done.14
  590.2 9.1 %collective-permute-done.15 = f32[32,1,768]{2,0,1:T(8,128)S(1)} collective-permute-done((f32[32,1,768]{2,0,1:T(8,128)S(1)}, f32[32,1,768]{2,0,1:T(8,128)S(1)}, u32[]{:S(2)}, u32[]{:S(2)}) %collective-permute-start.15) | collective-permute-done | bytes 98336 | tf_op jit(solution)/shard_map/ppermute | solution.py:17
  601.1 133.6 %all-reduce.9.cloned.1.call-done = f32[32,128,256]{2,1,0:T(8,128)} async-done(((f32[32,128,256]{2,1,0:T(8,128)}), f32[32,128,256]{2,1,0:T(8,128)}) %all-reduce.9.cloned.1.call-update) | async-done | bytes 4194320 | tf_op jit(solution)/shard_map/psum | solution.py:107
  734.7 3.6 fusion.180
  (189 shorter events, 60.4 us)
Async XLA Ops:
  7.2 183.6 %copy-start = (f32[32,32]{1,0:T(8,128)S(1)}, f32[32,32]{1,0:T(8,128)}, u32[]{:S(2)}) copy-start(f32[32,32]{1,0:T(8,128)} %param.11) | copy-start | bytes 12292
  7.2 166.4 %all-reduce.13.cloned.1.call-start = ((), (), s32[]{:S(2)}) async-start(), calls=%async_computation.3 | async-start | bytes 393216 | tf_op jit(solution)/shard_map/psum | solution.py:88
  8.4 169.4 %collective-permute-start = (f32[32,1,768]{2,0,1:T(8,128)S(1)}, f32[32,1,768]{2,0,1:T(8,128)}, u32[]{:S(2)}, u32[]{:S(2)}) collective-permute-start(f32[32,1,768]{2,0,1:T(8,128)S(1)} %slice.249), channel_id=1, source_target_pairs={{1,0},{2,1},{3,2},{4,3},{5,4},{6,5},{7,6},{8,7},{9,8},{10,9},{11,1... | collective-permute-start | bytes 294920 | tf_op jit(solution)/shard_map/ppermute | solution.py:17
  16.8 160.1 %collective-permute-start.6 = (f32[32,1,768]{2,0,1:T(8,128)}, f32[32,1,768]{2,0,1:T(8,128)}, u32[]{:S(2)}, u32[]{:S(2)}) collective-permute-start(f32[32,1,768]{2,0,1:T(8,128)} %slice.268), channel_id=1, source_target_pairs={{1,0},{2,1},{3,2},{4,3},{5,4},{6,5},{7,6},{8,7},{9,8},{10,9},{11,1... | collective-permute-start | bytes 294920 | tf_op jit(solution)/shard_map/ppermute | solution.py:17
  20.0 213.4 %copy-start.9 = (s32[128]{0:T(128)}, s32[128]{0:T(128)S(1)}, u32[]{:S(2)}) copy-start(s32[128]{0:T(128)S(1)} %iota_add_fusion.1) | copy-start | bytes 1540
  20.0 213.4 %copy-start.11 = (s32[3]{0:T(128)}, s32[3]{0:T(128)S(1)}, u32[]{:S(2)}) copy-start(s32[3]{0:T(128)S(1)} %iota_add_fusion) | copy-start | bytes 40
  26.7 152.0 %copy-start.2 = (f32[2,32,3,768]{3,1,2,0:T(8,128)S(1)}, f32[2,32,3,768]{3,1,2,0:T(8,128)}, u32[]{:S(2)}) copy-start(f32[2,32,3,768]{3,1,2,0:T(8,128)} %param.7) | copy-start | bytes 1769476
  32.7 347.0 %all-reduce.7.cloned.1.call-start = ((), (), s32[]{:S(2)}) async-start(), calls=%async_computation | async-start | bytes 8388608 | tf_op jit(solution)/shard_map/psum | solution.py:107
  32.7 147.5 %copy-start.13 = (pred[3]{0:T(512)(128)(4,1)}, pred[3]{0:T(512)(128)(4,1)S(1)}, u32[]{:S(2)}) copy-start(pred[3]{0:T(512)(128)(4,1)S(1)} %compare_and_fusion) | copy-start | bytes 13
  174.7 16.1 %copy-start.1 = (f32[2,32,3,768]{3,1,2,0:T(8,128)S(1)}, f32[2,32,3,768]{3,1,2,0:T(8,128)}, u32[]{:S(2)}) copy-start(f32[2,32,3,768]{3,1,2,0:T(8,128)} %param.10) | copy-start | bytes 1769476
  180.3 10.4 %collective-permute-start.1 = (f32[32,1,768]{2,0,1:T(8,128)S(1)}, f32[32,1,768]{2,0,1:T(8,128)S(1)}, u32[]{:S(2)}, u32[]{:S(2)}) collective-permute-start(f32[32,1,768]{2,0,1:T(8,128)S(1)} %slice.250), channel_id=1, source_target_pairs={{0,1},{1,2},{2,3},{3,4},{4,5},{5,6},{6,7},{7,8},{8,9},{9,10},{10,1... | collective-permute-start | bytes 294920 | tf_op jit(solution)/shard_map/ppermute | solution.py:17
  191.5 4.1 collective-permute-start.2
  195.7 10.5 %collective-permute-start.3 = (f32[32,1,768]{2,0,1:T(8,128)S(1)}, f32[32,1,768]{2,0,1:T(8,128)S(1)}, u32[]{:S(2)}, u32[]{:S(2)}) collective-permute-start(f32[32,1,768]{2,0,1:T(8,128)S(1)} %slice.256), channel_id=1, source_target_pairs={{0,1},{1,2},{2,3},{3,4},{4,5},{5,6},{6,7},{7,8},{8,9},{9,10},{10,1... | collective-permute-start | bytes 294920 | tf_op jit(solution)/shard_map/ppermute | solution.py:17
  206.9 4.1 collective-permute-start.4
  211.2 10.5 %collective-permute-start.5 = (f32[32,1,768]{2,0,1:T(8,128)S(1)}, f32[32,1,768]{2,0,1:T(8,128)S(1)}, u32[]{:S(2)}, u32[]{:S(2)}) collective-permute-start(f32[32,1,768]{2,0,1:T(8,128)S(1)} %slice.262), channel_id=1, source_target_pairs={{0,1},{1,2},{2,3},{3,4},{4,5},{5,6},{6,7},{7,8},{8,9},{9,10},{10,1... | collective-permute-start | bytes 294920 | tf_op jit(solution)/shard_map/ppermute | solution.py:17
  229.1 301.5 %all-reduce.11.cloned.1.call-start = ((), (), s32[]{:S(2)}) async-start(), calls=%async_computation.2 | async-start | bytes 393216 | tf_op jit(solution)/shard_map/psum | solution.py:88
  230.7 10.6 %collective-permute-start.7 = (f32[32,1,768]{2,0,1:T(8,128)S(1)}, f32[32,1,768]{2,0,1:T(8,128)S(1)}, u32[]{:S(2)}, u32[]{:S(2)}) collective-permute-start(f32[32,1,768]{2,0,1:T(8,128)S(1)} %slice.269), channel_id=1, source_target_pairs={{0,1},{1,2},{2,3},{3,4},{4,5},{5,6},{6,7},{7,8},{8,9},{9,10},{10,1... | collective-permute-start | bytes 294920 | tf_op jit(solution)/shard_map/ppermute | solution.py:17
  388.7 346.0 %all-reduce.9.cloned.1.call-start = ((), (), s32[]{:S(2)}) async-start(), calls=%async_computation.1 | async-start | bytes 8388608 | tf_op jit(solution)/shard_map/psum | solution.py:107
  390.3 142.2 %collective-permute-start.8 = (f32[32,1,768]{2,0,1:T(8,128)}, f32[32,1,768]{2,0,1:T(8,128)}, u32[]{:S(2)}, u32[]{:S(2)}) collective-permute-start(f32[32,1,768]{2,0,1:T(8,128)} %slice.275), channel_id=1, source_target_pairs={{1,0},{2,1},{3,2},{4,3},{5,4},{6,5},{7,6},{8,7},{9,8},{10,9},{11,1... | collective-permute-start | bytes 294920 | tf_op jit(solution)/shard_map/ppermute | solution.py:17
  534.6 17.5 %copy-start.6 = (f32[32,3,1]{2,0,1:T(8,128)S(1)}, f32[32,3,1]{2,0,1:T(8,128)}, u32[]{:S(2)}) copy-start(f32[32,3,1]{2,0,1:T(8,128)} %copy-done.5) | copy-start | bytes 1156
  536.4 15.6 %copy-start.4 = (f32[32,1,768]{2,0,1:T(8,128)S(1)}, f32[32,1,768]{2,0,1:T(8,128)}, u32[]{:S(2)}) copy-start(f32[32,1,768]{2,0,1:T(8,128)} %copy-done.3) | copy-start | bytes 294916
  536.6 10.7 %collective-permute-start.9 = (f32[32,1,768]{2,0,1:T(8,128)}, f32[32,1,768]{2,0,1:T(8,128)S(1)}, u32[]{:S(2)}, u32[]{:S(2)}) collective-permute-start(f32[32,1,768]{2,0,1:T(8,128)} %slice.276), channel_id=1, source_target_pairs={{0,1},{1,2},{2,3},{3,4},{4,5},{5,6},{6,7},{7,8},{8,9},{9,10},{10,1... | collective-permute-start | bytes 294920 | tf_op jit(solution)/shard_map/ppermute | solution.py:17
  547.9 4.1 collective-permute-start.10
  552.2 10.5 %collective-permute-start.11 = (f32[32,1,768]{2,0,1:T(8,128)S(1)}, f32[32,1,768]{2,0,1:T(8,128)S(1)}, u32[]{:S(2)}, u32[]{:S(2)}) collective-permute-start(f32[32,1,768]{2,0,1:T(8,128)S(1)} %slice.282), channel_id=1, source_target_pairs={{0,1},{1,2},{2,3},{3,4},{4,5},{5,6},{6,7},{7,8},{8,9},{9,10},{10,1... | collective-permute-start | bytes 294920 | tf_op jit(solution)/shard_map/ppermute | solution.py:17
  563.4 4.1 collective-permute-start.12
  567.6 10.5 %collective-permute-start.13 = (f32[32,1,768]{2,0,1:T(8,128)S(1)}, f32[32,1,768]{2,0,1:T(8,128)S(1)}, u32[]{:S(2)}, u32[]{:S(2)}) collective-permute-start(f32[32,1,768]{2,0,1:T(8,128)S(1)} %slice.288), channel_id=1, source_target_pairs={{0,1},{1,2},{2,3},{3,4},{4,5},{5,6},{6,7},{7,8},{8,9},{9,10},{10,1... | collective-permute-start | bytes 294920 | tf_op jit(solution)/shard_map/ppermute | solution.py:17
  579.5 8.5 %copy-start.7 = (f32[32,3,1]{2,0,1:T(8,128)S(1)}, f32[32,3,1]{2,0,1:T(8,128)}, u32[]{:S(2)}) copy-start(f32[32,3,1]{2,0,1:T(8,128)} %get-tuple-element.22) | copy-start | bytes 1156
  583.8 150.9 %copy-start.10 = (s32[128]{0:T(128)S(1)}, s32[128]{0:T(128)}, u32[]{:S(2)}) copy-start(s32[128]{0:T(128)} %copy-done.9) | copy-start | bytes 1540
  583.8 150.9 %copy-start.12 = (s32[3]{0:T(128)S(1)}, s32[3]{0:T(128)}, u32[]{:S(2)}) copy-start(s32[3]{0:T(128)} %copy-done.11) | copy-start | bytes 40
  583.9 4.1 collective-permute-start.14
  588.2 151.1 %copy-start.8 = (pred[3,768]{1,0:T(4,128)(4,1)S(1)}, pred[3,768]{1,0:T(4,128)(4,1)}, u32[]{:S(2)}) copy-start(pred[3,768]{1,0:T(4,128)(4,1)} %broadcast_and_fusion) | copy-start | bytes 6916
  588.2 11.1 %collective-permute-start.15 = (f32[32,1,768]{2,0,1:T(8,128)S(1)}, f32[32,1,768]{2,0,1:T(8,128)S(1)}, u32[]{:S(2)}, u32[]{:S(2)}) collective-permute-start(f32[32,1,768]{2,0,1:T(8,128)S(1)} %slice.294), channel_id=1, source_target_pairs={{0,1},{1,2},{2,3},{3,4},{4,5},{5,6},{6,7},{7,8},{8,9},{9,10},{10,1... | collective-permute-start | bytes 294920 | tf_op jit(solution)/shard_map/ppermute | solution.py:17
  (3 other events, 11.1 us)
Sparse Core Ops, SparseCore 0:
  32.8 140.7 all-reduce.12
  229.2 150.4 all-reduce.6
  388.8 141.6 all-reduce.10
  584.0 150.7 all-reduce.8
where the time goes:
time: 749 us; the launch traced here: 747 us
  waiting for transfers between devices  624 us (83%)
  starting transfers between devices  40.4 us (5%)
  local copies, waits for them, and re-layouts  31.3 us (4%)
  between operations  20.5 us (3%)
  matrix products  17.3 us (2%)
  other arithmetic  14.1 us (2%)
    psum x2, waiting for transfers between devices, per_device(): lax.psum((row_p, row_u, col_p, col_v), ('grp', 'tile'))  276 us
    psum x2, waiting for transfers between devices, per_device(): window = lax.psum(window, ('grp', 'tile'))  272 us
    ppermute x16, waiting for transfers between devices, passed_along(): lax.ppermute(value, axis, [(source, source + steps) for source in range(i...  75.5 us
    ppermute x16, starting transfers between devices, passed_along(): lax.ppermute(value, axis, [(source, source + steps) for source in range(i...  40.2 us
  transfers between devices with their start and end apart: 20, of which 17 were waited for; matrix products, arithmetic and copies ran while one was open for 3% of the time, Pallas kernels for 0%

commit v1 on v0

v1 whole, which is shorter than its diff:
```python
import functools

import jax
import jax.numpy as jnp
from jax import lax
from jax.experimental import pallas as pl
from jax.experimental.pallas import tpu as pltpu
from jax.sharding import PartitionSpec as P

RATIO = 3
OUTER = 2
COURANT = 0.3
MIXING = 0.15
STRIDE = 8
LAST_X0 = 60
MESH = pl.DeviceIdType.MESH
F32 = jnp.float32
BF16 = jnp.bfloat16


def pieces(x):
    a = x.astype(BF16)
    rest = x - a.astype(F32)
    b = rest.astype(BF16)
    c = (rest - b.astype(F32)).astype(BF16)
    return a, b, c


def kernel(
    n, tiles,
    row0_ref, col0_ref, vert_ref, p_in, u_in, v_in, k_in,
    p_out, u_out, v_out,
    n_p, n_u, n_v, n_k, p_p, p_u, p_v, p_k,
    n_ab, n_bl, n_ub, p_ab, p_bl, p_ub,
    g_send, g_mid, a_send, b_send, f_mid, a_row, b_row, fold,
    g_one0, g_one1, g_two0, g_two1, a_recv0, a_recv1, b_recv0, b_recv1, f_one0, f_one1, f_two0, f_two1,
    in_sem, out_sem, nx_send, nx_recv, px_send, px_recv,
    g1_send, g1_recv, g2_send, g2_recv, e_send, e_recv,
    f1_send, f1_recv, f2_send, f2_recv,
):
    levels, cols = n_k.shape[1], n_k.shape[2]
    win = cols // RATIO
    me = lax.axis_index("grp") * tiles + lax.axis_index("tile")
    first, last = me == 0, me == n - 1
    x0, y0 = row0_ref[0], col0_ref[0]
    shift_b, shift_c = lax.shift_right_logical(x0, 3), x0 & (STRIDE - 1)
    own = RATIO * me
    owners = (LAST_X0 + n) // RATIO + 1
    a_low = (1 + n) // RATIO
    a_count = owners - a_low
    b_count = (LAST_X0 - 1) // RATIO + 1
    finish = []
    g_one, g_two, a_recv, b_recv = (g_one0, g_one1), (g_two0, g_two1), (a_recv0, a_recv1), (b_recv0, b_recv1)
    f_one, f_two = (f_one0, f_one1), (f_two0, f_two1)

    def dev(d):
        return (d // tiles, d % tiles)

    def send(src, dst, s_sem, r_sem, to, cond=None, wait=True):
        copy = pltpu.make_async_remote_copy(
            src_ref=src, dst_ref=dst, send_sem=s_sem, recv_sem=r_sem, device_id=dev(to), device_id_type=MESH
        )
        if cond is None:
            copy.start()
            if wait:
                finish.append(copy.wait_send)
        else:
            pl.when(cond)(copy.start)
            if wait:
                finish.append(lambda: pl.when(cond)(copy.wait_send))

    def arrived(ref, sem, cond=None):
        def go():
            pltpu.make_async_copy(ref, ref, sem).wait()
        if cond is None:
            go()
        else:
            pl.when(cond)(go)

    loads = {}
    for at, (name, src, g, dst) in enumerate((
        ("pp", p_in, 0, p_p.at[0]), ("pv", v_in, 0, p_v), ("pu", u_in, 0, p_u),
        ("np", p_in, 1, n_p.at[0]), ("nu", u_in, 1, n_u), ("nv", v_in, 1, n_v),
        ("nk", k_in, 1, n_k), ("pk", k_in, 0, p_k),
    )):
        loads[name] = pltpu.make_async_copy(src.at[g], dst, in_sem.at[at])
        loads[name].start()

    def exchange(src, s, ab, bl, ss, rs):
        send(src.at[2], bl.at[s], ss.at[2 * s], rs.at[2 * s], me + 1, ~last)
        send(src.at[0], ab.at[s], ss.at[2 * s + 1], rs.at[2 * s + 1], me - 1, ~first)

    exchange(p_in.at[1], 0, n_ab, n_bl, nx_send, nx_recv)
    send(u_in.at[1, 2], n_ub, nx_send.at[12], nx_recv.at[12], me + 1, ~last)

    lane = lax.broadcasted_iota(jnp.int32, (levels, cols), 1)
    lane128 = lax.broadcasted_iota(jnp.int32, (levels, 128), 1)
    level128 = lax.broadcasted_iota(jnp.int32, (levels, 128), 0)

    def valid_edges():
        for w in range(2):
            base = me + n * w
            for m in range(4):
                owner = base // RATIO + m
                slot = base % RATIO + 7 - RATIO * m
                cond = (slot >= 0) & (owner < owners)
                if w == 1:
                    cond = cond & (me < 8 * STRIDE)
                yield owner, cond, slot, 4 * w + m

    def start_ghosts(o, pp):
        gsum = jnp.zeros((8, 128), F32)
        row8 = lax.broadcasted_iota(jnp.int32, (8, 128), 0)
        for j in range(RATIO):
            right = jnp.sum(jnp.where(lane == y0 + win, pp[j], 0.0), axis=1, keepdims=True)
            left = jnp.sum(jnp.where(lane == y0 - 1, p_v[j], 0.0), axis=1, keepdims=True)
            both = jnp.where(level128 == lane128, right, 0.0) + jnp.where(level128 == lane128 - levels, left, 0.0)
            gsum = jnp.where(row8 == j, jnp.sum(both, axis=0, keepdims=True), gsum)
        g_send[o] = gsum
        for k in range(10):
            base = own + k - 7
            m = -((k - 7) // RATIO)
            slot = 4 * (base // n) + m
            to = base % n
            cond = (base >= 0) & (me < owners)
            pick = g_one[o].at[jnp.clip(slot, 0, 7)]

            @pl.when(cond & (to == me))
            def _():
                g_one[o][jnp.clip(slot, 0, 7)] = g_send[o]
            send(g_send.at[o], pick, g1_send.at[o, k], g1_recv.at[o, jnp.clip(slot, 0, 7)], to, cond & (to != me))

        def pick_row(field, target):
            out = jnp.zeros((levels, cols), F32)
            for j in range(RATIO):
                out = jnp.where(target == own + j, field[j], out)
            return pltpu.roll(out, cols - y0, axis=1)[:, :win]

        is_a = (me >= a_low) & (me < owners)
        is_b = me < b_count

        @pl.when(is_a)
        def _():
            a_send[o] = pick_row(pp, x0 + n)
        send(a_send.at[o], a_recv[o].at[jnp.clip(me - a_low, 0, a_count - 1)], e_send.at[o, 0], e_recv.at[o, 0], n - 1, is_a)

        @pl.when(is_b)
        def _():
            b_send[o] = pick_row(p_u, x0 - 1)

        @pl.when(first)
        def _():
            b_recv[o][0] = b_send[o]
        send(b_send.at[o], b_recv[o].at[jnp.clip(me, 0, b_count - 1)], e_send.at[o, 1], e_recv.at[o, 1], 0, is_b & ~first)

    def pass_ghosts(o):
        for owner, cond, _, here in valid_edges():
            arrived(g_one[o].at[here], g1_recv.at[o, here], cond & (owner != me))
        wrapped = me < STRIDE * shift_b
        rem = jnp.where(wrapped, (me + n) % RATIO, me % RATIO) + shift_c
        slot = jnp.where(wrapped, 4, 0) + rem // RATIO
        row8 = lax.broadcasted_iota(jnp.int32, (8, 128), 0)
        block = g_one[o][slot]
        row = jnp.sum(jnp.where(row8 == rem % RATIO, block, 0.0), axis=0, keepdims=True)
        g_mid[o] = jnp.broadcast_to(row, (8, 128))
        g_two[o][0] = jnp.broadcast_to(row, (8, 128))
        for b in range(1, 8):
            send(g_mid.at[o], g_two[o].at[b], g2_send.at[o], g2_recv.at[o], (me + n - STRIDE * b) % n, wait=False)
        finish.append(lambda: arrived(g_two[o].at[pl.ds(1, 7)], g2_send.at[o]))

    def take_ghosts(o):
        arrived(g_two[o].at[pl.ds(1, 7)], g2_recv.at[o])
        row = g_two[o][shift_b][0:1]
        right = jnp.sum(jnp.where(level128 == lane128, row, 0.0), axis=1, keepdims=True)
        left = jnp.sum(jnp.where(level128 == lane128 - levels, row, 0.0), axis=1, keepdims=True)

        def widen(x):
            a, b, c = pieces(x)
            stack = jnp.concatenate([a, b, c], axis=0)
            wide = lax.dot_general(stack, fold[...], (((1,), (1,)), ((), ())), preferred_element_type=F32)
            return (wide[:levels] + wide[levels:2 * levels]) + wide[2 * levels:]

        @pl.when(last)
        def _():
            arrived(a_recv[o], e_recv.at[o, 0])
            a_row[...] = widen(a_recv[o][jnp.clip((x0 + n) // RATIO - a_low, 0, a_count - 1)])

        @pl.when(first)
        def _():
            arrived(b_recv[o].at[pl.ds(1, b_count - 1)], e_recv.at[o, 1])
            b_row[...] = widen(b_recv[o][jnp.clip((x0 - 1) // RATIO, 0, b_count - 1)])
            n_ub[...] = b_row[...]

        return jnp.broadcast_to(right, (levels, 128)), jnp.broadcast_to(left, (levels, 128))

    def from_right(x, edge):
        moved = pltpu.roll(x, cols - 1, axis=1)
        if edge is None:
            return moved
        tail = jnp.where(lane128 == 127, edge, moved[:, cols - 128:])
        return jnp.concatenate([moved[:, :cols - 128], tail], axis=1)

    def from_left(x, edge):
        moved = pltpu.roll(x, 1, axis=1)
        if edge is None:
            return moved
        head = jnp.where(lane128 == 0, edge, moved[:, :128])
        return jnp.concatenate([head, moved[:, 128:]], axis=1)

    def mixed(q, mix):
        a, b, c = pieces(q)
        return q + jnp.dot(mix, jnp.concatenate([a, b, a, b, c, a], axis=0), preferred_element_type=F32)

    def new_pressure(p, k, u, below, v, left, mix):
        return mixed(p - COURANT * k * ((u - below) + (v - from_left(v, left))), mix)

    def nest_substep(s, right, left, mix):
        p, new = n_p.at[s], n_p.at[s + 1]
        for r in range(RATIO):
            n_v[r] = n_v[r] - COURANT * (from_right(p[r], right) - p[r])
        for r in range(2):
            n_u[r] = n_u[r] - COURANT * (p[r + 1] - p[r])
        arrived(n_bl.at[s], nx_recv.at[2 * s], ~first)
        if s == 0:
            arrived(n_ub, nx_recv.at[12], ~first)

        @pl.when(~first)
        def _():
            n_ub[...] = n_ub[...] - COURANT * (p[0] - n_bl[s])
        new[0] = new_pressure(p[0], n_k[0], n_u[0], n_ub[...], n_v[0], left, mix)
        if s < 5:
            send(new.at[0], n_ab.at[s + 1], nx_send.at[2 * s + 3], nx_recv.at[2 * s + 3], me - 1, ~first)

        arrived(n_ab.at[s], nx_recv.at[2 * s + 1], ~last)

        @pl.when(last)
        def _():
            n_ab[s] = a_row[...]
        n_u[2] = n_u[2] - COURANT * (n_ab[s] - p[2])
        new[2] = new_pressure(p[2], n_k[2], n_u[2], n_u[1], n_v[2], left, mix)
        if s < 5:
            send(new.at[2], n_bl.at[s + 1], nx_send.at[2 * s + 2], nx_recv.at[2 * s + 2], me + 1, ~last)
        new[1] = new_pressure(p[1], n_k[1], n_u[1], n_u[0], n_v[1], left, mix)

    def parent_substep(s, mix):
        p, new = p_p.at[s], p_p.at[s + 1]
        arrived(p_bl.at[s], px_recv.at[2 * s], ~first)
        arrived(p_ab.at[s], px_recv.at[2 * s + 1], ~last)
        if s == 0:
            arrived(p_ub, px_recv.at[4], ~first)
        for r in range(RATIO):
            p_v[r] = p_v[r] - COURANT * (from_right(p[r], None) - p[r])
        for r in range(2):
            p_u[r] = p_u[r] - COURANT * (p[r + 1] - p[r])
        p_u[2] = jnp.where(last, 0.0, p_u[2] - COURANT * (p_ab[s] - p[2]))
        p_ub[...] = jnp.where(first, 0.0, p_ub[...] - COURANT * (p[0] - p_bl[s]))
        for r in range(RATIO):
            below = p_ub[...] if r == 0 else p_u[r - 1]
            new[r] = new_pressure(p[r], p_k[r], p_u[r], below, p_v[r], None, mix)

    def start_feedback(o):
        rows = n_p.at[3 * (o + 1)]
        a, b, c = pieces((rows[0] + rows[1]) + rows[2])
        stack = jnp.concatenate([a, b, c], axis=0)
        mean = jnp.dot(stack, fold[...], preferred_element_type=F32)
        mean = ((mean[:levels] + mean[levels:2 * levels]) + mean[2 * levels:]) * (1.0 / (RATIO * RATIO))
        f_one[o][0] = mean
        for b in range(1, 8):
            send(f_one[o].at[0], f_one[o].at[b], f1_send.at[o], f1_recv.at[o], (me + STRIDE * b) % n, wait=False)
        finish.append(lambda: arrived(f_one[o].at[pl.ds(1, 7)], f1_send.at[o]))

    def pass_feedback(o):
        arrived(f_one[o].at[pl.ds(1, 7)], f1_recv.at[o])
        f_mid[o] = f_one[o][shift_b]
        for owner, cond, slot, here in valid_edges():
            slot = jnp.clip(slot, 0, 9)

            @pl.when(cond & (owner == me))
            def _():
                f_two[o][slot] = f_mid[o]
            send(f_mid.at[o], f_two[o].at[slot], f2_send.at[o, here], f2_recv.at[o, slot], owner % n, cond & (owner != me))

    def take_feedback(o, pp):
        for k in range(10):
            base = own + k - 7
            arrived(f_two[o].at[k], f2_recv.at[o, k], (base >= 0) & (me < owners) & (base % n != me))
        under = (lane >= y0) & (lane < y0 + win)
        for j in range(RATIO):
            row = own + j
            value = f_two[o][j - shift_c + 7]
            value = pltpu.roll(jnp.concatenate([value, jnp.zeros((levels, cols - win), F32)], axis=1), y0, axis=1)
            inside = ((row >= x0) & (row < x0 + n)).astype(jnp.int32)
            pp[j] = jnp.where(under & (jnp.broadcast_to(inside, (levels, cols)) > 0), value, pp[j])

    exchange(p_in.at[0], 0, p_ab, p_bl, px_send, px_recv)
    send(u_in.at[0, 2], p_ub, px_send.at[4], px_recv.at[4], me + 1, ~last)
    for name in ("pp", "pv", "pu"):
        loads[name].wait()
    start_ghosts(0, p_p.at[0])

    spot = lax.broadcasted_iota(jnp.int32, (cols, win), 0) - RATIO * lax.broadcasted_iota(jnp.int32, (cols, win), 1)
    fold[...] = jnp.where((spot >= 0) & (spot < RATIO), 1.0, 0.0).astype(BF16)
    block = lax.broadcasted_iota(jnp.int32, (levels, 6 * levels), 1)
    copies = (block % levels == lax.broadcasted_iota(jnp.int32, (levels, 6 * levels), 0)).astype(F32)
    wide = jnp.dot(MIXING * vert_ref[...], copies, precision=lax.Precision.HIGHEST, preferred_element_type=F32)
    m1, m2, m3 = (x.astype(F32) for x in pieces(wide))
    part = block // levels
    mix = jnp.where(part >= 5, m3, jnp.where((part == 2) | (part == 3), m2, m1)).astype(BF16)

    pass_ghosts(0)
    for name in ("np", "nu", "nv", "nk", "pk"):
        loads[name].wait()
    right, left = take_ghosts(0)
    nest_substep(0, right, left, mix)
    parent_substep(0, mix)
    start_ghosts(1, p_p.at[1])
    nest_substep(1, right, left, mix)
    pass_ghosts(1)
    nest_substep(2, right, left, mix)
    start_feedback(0)
    right, left = take_ghosts(1)
    nest_substep(3, right, left, mix)
    pass_feedback(0)
    nest_substep(4, right, left, mix)
    take_feedback(0, p_p.at[1])
    exchange(p_p.at[1], 1, p_ab, p_bl, px_send, px_recv)
    nest_substep(5, right, left, mix)
    start_feedback(1)
    outs = []

    def store(src, dst):
        outs.append(pltpu.make_async_copy(src, dst, out_sem.at[len(outs)]))
        outs[-1].start()
    store(n_p.at[6], p_out.at[1])
    store(n_u, u_out.at[1])
    store(n_v, v_out.at[1])
    parent_substep(1, mix)
    store(p_u, u_out.at[0])
    store(p_v, v_out.at[0])
    pass_feedback(1)
    take_feedback(1, p_p.at[2])
    store(p_p.at[2], p_out.at[0])
    for wait in finish:
        wait()
    for copy in outs:
        copy.wait()


def per_device(n, tiles, pressure, u_wind, v_wind, stiffness, vertical, nest_row0, nest_col0):
    fields = [jnp.transpose(x, (0, 2, 1, 3)) for x in (pressure, u_wind, v_wind, stiffness)]
    _, rows, levels, cols = fields[0].shape
    win = cols // RATIO
    slab = (rows, levels, cols)
    row = (levels, cols)
    owners = (LAST_X0 + n) // RATIO + 1
    a_count = owners - (1 + n) // RATIO
    b_count = (LAST_X0 - 1) // RATIO + 1
    vmem = lambda *shape: pltpu.VMEM(shape, F32)
    dma = lambda *shape: pltpu.SemaphoreType.DMA(shape)
    outs = pl.pallas_call(
        functools.partial(kernel, n, tiles),
        out_shape=[jax.ShapeDtypeStruct((2,) + slab, F32)] * 3,
        in_specs=[pl.BlockSpec(memory_space=pltpu.SMEM)] * 2
        + [pl.BlockSpec(memory_space=pltpu.VMEM)]
        + [pl.BlockSpec(memory_space=pl.ANY)] * 4,
        out_specs=[pl.BlockSpec(memory_space=pl.ANY)] * 3,
        scratch_shapes=[
            vmem(7, *slab), vmem(*slab), vmem(*slab), vmem(*slab),
            vmem(3, *slab), vmem(*slab), vmem(*slab), vmem(*slab),
            vmem(6, *row), vmem(6, *row), vmem(*row), vmem(2, *row), vmem(2, *row), vmem(*row),
            vmem(OUTER, 8, 128), vmem(OUTER, 8, 128), vmem(OUTER, levels, win), vmem(OUTER, levels, win),
            vmem(OUTER, levels, win), vmem(*row), vmem(*row), pltpu.VMEM((cols, win), BF16),
            *[vmem(8, 8, 128)] * 4,
            *[vmem(a_count, levels, win)] * 2, *[vmem(b_count, levels, win)] * 2,
            *[vmem(8, levels, win)] * 2, *[vmem(10, levels, win)] * 2,
            dma(8), dma(6), dma(13), dma(13), dma(5), dma(5),
            dma(OUTER, 10), dma(OUTER, 8), dma(OUTER), dma(OUTER), dma(OUTER, 2), dma(OUTER, 2),
            dma(OUTER), dma(OUTER), dma(OUTER, 8), dma(OUTER, 10),
        ],
        compiler_params=pltpu.CompilerParams(has_side_effects=True, vmem_limit_bytes=48 * 1024 * 1024),
        cost_estimate=pl.CostEstimate(flops=300_000_000, bytes_accessed=4_200_000, transcendentals=0),
    )(nest_row0, nest_col0, vertical, *fields)
    return tuple(jnp.transpose(x, (0, 2, 1, 3)) for x in outs)


def solution(mesh):
    spec = P(None, None, ("grp", "tile"), None)
    tiles = mesh.shape["tile"]
    return jax.shard_map(
        functools.partial(per_device, mesh.shape["grp"] * tiles, tiles),
        mesh=mesh,
        in_specs=(spec, spec, spec, spec, P(), P(), P()),
        out_specs=(spec, spec, spec),
        check_vma=False,
    )
```

time: 749 us -> 80.4 us (0.11)
  waiting for transfers between devices: 624 us -> 0 us
  Pallas kernels: 0 us -> 71 us
  starting transfers between devices: 40.4 us -> 0 us
  local copies, waits for them, and re-layouts: 31.3 us -> 8.09 us
  between operations: 20.5 us -> 0.66 us
  matrix products: 17.3 us -> 0 us
  other arithmetic: 14.1 us -> 0 us
    psum x4 -> x0, waiting for transfers between devices: 548 us -> none  [the longest x2 276 us: per_device(): lax.psum((row_p, row_u, col_p, col_v), ('grp', 'tile'))]
    ppermute x16 -> x0, waiting for transfers between devices: 75.5 us -> none  [passed_along(): lax.ppermute(value, axis, [(source, source + steps) for source in range(i...]
    pallas_call x0 -> x1, Pallas kernels: none -> 71 us  [per_device(): pl.pallas_call(functools.partial(kernel, n, tiles), out_shape=[jax.ShapeD...]
    ppermute x16 -> x0, starting transfers between devices: 40.2 us -> none  [passed_along(): lax.ppermute(value, axis, [(source, source + steps) for source in range(i...]
    dot_general x14 -> x0, matrix products: 17.3 us -> none  [the longest x2 7.27 us: per_device(): jnp.einsum('ri,lrc->lic', selector, window, precision=lax.Precision.HIGHEST)]
    slice x46 -> x0, local copies, waits for them, and re-layouts: 8.01 us -> none  [the longest x8 1.8 us: substep(): p_rt = jnp.concatenate([p_field[:, :, 1:], right], axis=2)]
    unnamed x30 -> x17, local copies, waits for them, and re-layouts: 0.08 us -> 8.09 us
  transfers between devices with their start and end apart: 20 -> 0, of which waited for: 17 -> 0; matrix products, arithmetic and copies ran while one was open for 3% -> 0% of each run, Pallas kernels for 0% -> 0%
where the time goes in v1:
time: 80.4 us; the launch traced here: 79.7 us
  Pallas kernels  71 us (88%)
  local copies, waits for them, and re-layouts  8.09 us (10%)
    pallas_call x1, Pallas kernels, per_device(): pl.pallas_call(functools.partial(kernel, n, tiles), out_shape=[jax.ShapeD...  71 us
    unnamed x17, local copies, waits for them, and re-layouts  8.09 us

profile of v1, /device:TPU:8, one launch (start us, length us, event | category | flops | bytes accessed | tf_op | source)
XLA Modules:
  0.0 79.7 jit_solution(7789133552707397926)
XLA Ops:
  0.6 0.0 copy-start.5
  0.6 0.0 copy-start.6
  0.7 0.7 copy-done.5
  1.3 0.0 copy-done.6
  1.3 0.0 copy-start
  1.3 1.1 %copy-done = f32[2,32,3,768]{3,1,2,0:T(8,128)S(1)} copy-done((f32[2,32,3,768]{3,1,2,0:T(8,128)S(1)}, f32[2,32,3,768]{3,1,2,0:T(8,128)}, u32[]{:S(2)}) %copy-start) | copy-done | bytes 589848
  2.4 0.0 copy-start.1
  2.4 1.1 %copy-done.1 = f32[2,32,3,768]{3,1,2,0:T(8,128)S(1)} copy-done((f32[2,32,3,768]{3,1,2,0:T(8,128)S(1)}, f32[2,32,3,768]{3,1,2,0:T(8,128)}, u32[]{:S(2)}) %copy-start.1) | copy-done | bytes 589848
  3.4 0.0 copy-start.2
  3.5 1.1 %copy-done.2 = f32[2,32,3,768]{3,1,2,0:T(8,128)S(1)} copy-done((f32[2,32,3,768]{3,1,2,0:T(8,128)S(1)}, f32[2,32,3,768]{3,1,2,0:T(8,128)}, u32[]{:S(2)}) %copy-start.2) | copy-done | bytes 589848
  4.5 0.0 copy-start.3
  4.5 1.1 %copy-done.3 = f32[2,32,3,768]{3,1,2,0:T(8,128)S(1)} copy-done((f32[2,32,3,768]{3,1,2,0:T(8,128)S(1)}, f32[2,32,3,768]{3,1,2,0:T(8,128)}, u32[]{:S(2)}) %copy-start.3) | copy-done | bytes 589848
  5.6 0.0 copy-start.4
  5.6 0.7 copy-done.4
  6.3 71.0 %shard_map.94 = (f32[2,3,32,768]{3,2,1,0:T(8,128)S(1)}, f32[2,3,32,768]{3,2,1,0:T(8,128)S(1)}, f32[2,3,32,768]{3,2,1,0:T(8,128)S(1)}) custom-call(s32[60]{0:T(128)S(1)} %copy-done.6, s32[511]{0:T(512)S(1)} %copy-done.5, f32[32,32]{1,0:T(8,128)S(1)} %copy-done.4, f32[2,3,32,768]{3,2,1,0:T(8,128)S(1)} %bitcast.10, f32[2,3,32,768]{3,2,1,0:T(8,128)S(1)} %bitcast.11, ...), custom_call_target="tpu_custom_call" | custom-call | flops 300000000 | bytes 4200000 | tf_op jit(solution)/shard_map/pallas_call | solution.py:360
  77.3 0.8 %copy.13 = f32[2,32,3,768]{3,1,2,0:T(8,128)} copy(f32[2,32,3,768]{3,1,2,0:T(8,128)S(1)} %bitcast.9) | data formatting | bytes 1179648
  78.1 0.8 %copy.14 = f32[2,32,3,768]{3,1,2,0:T(8,128)} copy(f32[2,32,3,768]{3,1,2,0:T(8,128)S(1)} %bitcast.8) | data formatting | bytes 1179648
  78.9 0.8 %copy.15 = f32[2,32,3,768]{3,1,2,0:T(8,128)} copy(f32[2,32,3,768]{3,1,2,0:T(8,128)S(1)} %bitcast.7) | data formatting | bytes 1179648
Async XLA Ops:
  0.6 0.7 copy-start.5
  0.6 0.7 copy-start.6
  1.3 1.1 %copy-start = (f32[2,32,3,768]{3,1,2,0:T(8,128)S(1)}, f32[2,32,3,768]{3,1,2,0:T(8,128)}, u32[]{:S(2)}) copy-start(f32[2,32,3,768]{3,1,2,0:T(8,128)} %param.7) | copy-start | bytes 1769476
  2.4 1.1 %copy-start.1 = (f32[2,32,3,768]{3,1,2,0:T(8,128)S(1)}, f32[2,32,3,768]{3,1,2,0:T(8,128)}, u32[]{:S(2)}) copy-start(f32[2,32,3,768]{3,1,2,0:T(8,128)} %param.8) | copy-start | bytes 1769476
  3.4 1.1 %copy-start.2 = (f32[2,32,3,768]{3,1,2,0:T(8,128)S(1)}, f32[2,32,3,768]{3,1,2,0:T(8,128)}, u32[]{:S(2)}) copy-start(f32[2,32,3,768]{3,1,2,0:T(8,128)} %param.9) | copy-start | bytes 1769476
  4.5 1.1 %copy-start.3 = (f32[2,32,3,768]{3,1,2,0:T(8,128)S(1)}, f32[2,32,3,768]{3,1,2,0:T(8,128)}, u32[]{:S(2)}) copy-start(f32[2,32,3,768]{3,1,2,0:T(8,128)} %param.10) | copy-start | bytes 1769476
  5.6 0.7 copy-start.4

commit v2 on v1

v2 whole, which is shorter than its diff:
```python
import functools

import jax
import jax.numpy as jnp
from jax import lax
from jax.experimental import pallas as pl
from jax.experimental.pallas import tpu as pltpu
from jax.sharding import PartitionSpec as P

RATIO = 3
OUTER = 2
COURANT = 0.3
MIXING = 0.15
STRIDE = 8
LAST_X0 = 60
MESH = pl.DeviceIdType.MESH
F32 = jnp.float32
BF16 = jnp.bfloat16


def pieces(x):
    a = x.astype(BF16)
    rest = x - a.astype(F32)
    b = rest.astype(BF16)
    c = (rest - b.astype(F32)).astype(BF16)
    return a, b, c


def kernel(
    n, tiles,
    row0_ref, col0_ref, vert_ref, p_in, u_in, v_in, k_in,
    p_out, u_out, v_out,
    n_p, n_u, n_v, n_k, p_p, p_u, p_v, p_k,
    g_send, g_mid, a_send, b_send, f_mid, a_row, b_row, edge, fold, mix,
    g_one0, g_one1, g_two0, g_two1, a_recv0, a_recv1, b_recv0, b_recv1, f_one0, f_one1, f_two0, f_two1,
    in_sem, out_sem, ni_send, ni_recv, nx_send, nx_recv, nm_send, nm_recv, px_send, px_recv,
    g1_send, g1_recv, g2_send, g2_recv, e_send, e_recv,
    f1_send, f1_recv, f2_send, f2_recv,
):
    levels, cols = n_k.shape[1], n_k.shape[2]
    win = cols // RATIO
    me = lax.axis_index("grp") * tiles + lax.axis_index("tile")
    first, last = me == 0, me == n - 1
    x0, y0 = row0_ref[0], col0_ref[0]
    shift_b, shift_c = lax.shift_right_logical(x0, 3), x0 & (STRIDE - 1)
    own = RATIO * me
    owners = (LAST_X0 + n) // RATIO + 1
    a_low = (1 + n) // RATIO
    a_count = owners - a_low
    b_count = (LAST_X0 - 1) // RATIO + 1
    finish = []
    g_one, g_two, a_recv, b_recv = (g_one0, g_one1), (g_two0, g_two1), (a_recv0, a_recv1), (b_recv0, b_recv1)
    f_one, f_two = (f_one0, f_one1), (f_two0, f_two1)

    def dev(d):
        return (d // tiles, d % tiles)

    def remote(src, dst, s_sem, r_sem, to):
        return pltpu.make_async_remote_copy(
            src_ref=src, dst_ref=dst, send_sem=s_sem, recv_sem=r_sem, device_id=dev(to), device_id_type=MESH
        )

    def send(src, dst, s_sem, r_sem, to, cond):
        copy = remote(src, dst, s_sem, r_sem, to)
        pl.when(cond)(copy.start)
        finish.append(lambda: pl.when(cond)(copy.wait_send))

    def loop(low, high, body):
        lax.fori_loop(low, high, lambda i, _: (body(i), 0)[1], 0)

    def send_each(count, make):
        def start(i):
            copy, cond = make(i)
            pl.when(cond)(copy.start)

        def end(i):
            copy, cond = make(i)
            pl.when(cond)(copy.wait_send)
        loop(0, count, start)
        finish.append(lambda: loop(0, count, end))

    def arrived(ref, sem, cond=True):
        @pl.when(cond)
        def _():
            pltpu.make_async_copy(ref, ref, sem).wait()

    loads = {}
    for at, (name, src, g, dst) in enumerate((
        ("pp", p_in, 0, p_p.at[0, pl.ds(1, 3)]), ("pv", v_in, 0, p_v), ("pu", u_in, 0, p_u.at[pl.ds(1, 3)]),
        ("np", p_in, 1, n_p.at[0, pl.ds(2, 3)]), ("nu", u_in, 1, n_u.at[pl.ds(2, 3)]),
        ("nv", v_in, 1, n_v.at[pl.ds(1, 3)]), ("nk", k_in, 1, n_k.at[pl.ds(1, 3)]), ("pk", k_in, 0, p_k),
    )):
        loads[name] = pltpu.make_async_copy(src.at[g], dst, in_sem.at[at])
        loads[name].start()

    def parent_exchange(s, rows):
        send(rows.at[2], p_p.at[s, 0], px_send.at[s, 0], px_recv.at[s, 0], me + 1, ~last)
        send(rows.at[0], p_p.at[s, 4], px_send.at[s, 1], px_recv.at[s, 1], me - 1, ~first)

    parent_exchange(0, p_in.at[0])
    send(u_in.at[0, 2], p_u.at[0], px_send.at[0, 2], px_recv.at[0, 2], me + 1, ~last)
    to_up = (
        (p_in.at[1, pl.ds(1, 2)], n_p.at[0, pl.ds(0, 2)]), (u_in.at[1, pl.ds(1, 2)], n_u.at[pl.ds(0, 2)]),
        (v_in.at[1, 2], n_v.at[0]), (k_in.at[1, 2], n_k.at[0]),
    )
    to_down = (
        (p_in.at[1, pl.ds(0, 2)], n_p.at[0, pl.ds(5, 2)]), (u_in.at[1, 0], n_u.at[5]),
        (v_in.at[1, 0], n_v.at[4]), (k_in.at[1, 0], n_k.at[4]),
    )
    for i in range(4):
        send(*to_up[i], ni_send.at[0, i], ni_recv.at[0, i], me + 1, ~last)
        send(*to_down[i], ni_send.at[1, i], ni_recv.at[1, i], me - 1, ~first)

    lane = lax.broadcasted_iota(jnp.int32, (levels, cols), 1)
    lane128 = lax.broadcasted_iota(jnp.int32, (levels, 128), 1)
    level128 = lax.broadcasted_iota(jnp.int32, (levels, 128), 0)
    row8 = lax.broadcasted_iota(jnp.int32, (8, 128), 0)

    def start_ghosts(o, pp, pu):
        def gather(j, total):
            right = jnp.sum(jnp.where(lane == y0 + win, pp[j], 0.0), axis=1, keepdims=True)
            left = jnp.sum(jnp.where(lane == y0 - 1, p_v[j], 0.0), axis=1, keepdims=True)
            both = jnp.where(level128 == lane128, right, 0.0) + jnp.where(level128 == lane128 - levels, left, 0.0)
            return jnp.where(row8 == j, jnp.sum(both, axis=0, keepdims=True), total)
        g_send[o] = lax.fori_loop(0, RATIO, gather, jnp.zeros((8, 128), F32))

        def column(k):
            base = own + k - STRIDE
            slot = jnp.where(base >= n, 4, 0) + 3 - k // RATIO
            to = (base + n) % n
            cond = (base >= 0) & (me < owners)

            @pl.when(cond & (to == me))
            def _():
                g_one[o][slot] = g_send[o]
            copy = remote(g_send.at[o], g_one[o].at[slot], g1_send.at[o, k], g1_recv.at[o, slot], to)
            return copy, cond & (to != me)
        send_each(STRIDE + 4, column)

        def pick_row(field, target):
            out = jnp.zeros((levels, cols), F32)
            for j in range(RATIO):
                out = jnp.where(target == own + j, field[j], out)
            return pltpu.roll(out, cols - y0, axis=1)[:, :win]

        is_a = (me >= a_low) & (me < owners)
        is_b = me < b_count

        @pl.when(is_a)
        def _():
            a_send[o] = pick_row(pp, x0 + n)
        send(a_send.at[o], a_recv[o].at[jnp.clip(me - a_low, 0, a_count - 1)], e_send.at[o, 0], e_recv.at[o, 0], n - 1, is_a)

        @pl.when(is_b)
        def _():
            b_send[o] = pick_row(pu, x0 - 1)

        @pl.when(first)
        def _():
            b_recv[o][0] = b_send[o]
        send(b_send.at[o], b_recv[o].at[jnp.clip(me, 0, b_count - 1)], e_send.at[o, 1], e_recv.at[o, 1], 0, is_b & ~first)

    def pass_ghosts(o):
        for w in range(2):
            base = me + n * w
            for m in range(4):
                owner = (base + 2) // RATIO - 1 + m
                cond = (owner >= 0) & (owner < owners) & (owner != me)
                if w == 1:
                    cond = cond & (me < 8 * STRIDE)
                arrived(g_one[o].at[4 * w + m], g1_recv.at[o, 4 * w + m], cond)
        wrapped = me < STRIDE * shift_b
        rem = jnp.where(wrapped, (me + n + 2) % RATIO, (me + 2) % RATIO) + shift_c
        rows = jnp.zeros((8, 128), F32)
        for t in range(3):
            block = g_one[o][jnp.where(wrapped, 4, 0) + (rem + t) // RATIO]
            row = jnp.sum(jnp.where(row8 == (rem + t) % RATIO, block, 0.0), axis=0, keepdims=True)
            rows = jnp.where(row8 == t, row, rows)
        g_mid[o] = rows
        g_two[o][0] = rows

        def onward(i):
            b = i + 1
            return remote(g_mid.at[o], g_two[o].at[b], g2_send.at[o, i], g2_recv.at[o], (me + n - STRIDE * b) % n), True
        send_each(7, onward)

    def take_ghosts(o):
        arrived(g_two[o].at[pl.ds(1, 7)], g2_recv.at[o])
        rows = g_two[o][shift_b]
        for t in range(3):
            row = rows[t:t + 1]
            right = jnp.sum(jnp.where(level128 == lane128, row, 0.0), axis=1, keepdims=True)
            left = jnp.sum(jnp.where(level128 == lane128 - levels, row, 0.0), axis=1, keepdims=True)
            edge[t, 0] = jnp.broadcast_to(right, (levels, 128))
            edge[t, 1] = jnp.broadcast_to(left, (levels, 128))

        def widen(x):
            a, b, c = pieces(x)
            stack = jnp.concatenate([a, b, c], axis=0)
            wide = lax.dot_general(stack, fold[...], (((1,), (1,)), ((), ())), preferred_element_type=F32)
            return (wide[:levels] + wide[levels:2 * levels]) + wide[2 * levels:]

        @pl.when(last)
        def _():
            arrived(a_recv[o], e_recv.at[o, 0])
            a_row[...] = widen(a_recv[o][jnp.clip((x0 + n) // RATIO - a_low, 0, a_count - 1)])

        @pl.when(first)
        def _():
            arrived(b_recv[o].at[pl.ds(1, b_count - 1)], e_recv.at[o, 1])
            b_row[...] = widen(b_recv[o][jnp.clip((x0 - 1) // RATIO, 0, b_count - 1)])

    def from_right(x, ghost):
        moved = pltpu.roll(x, cols - 1, axis=1)
        if ghost is None:
            return moved
        tail = jnp.where(lane128 == 127, ghost, moved[:, cols - 128:])
        return jnp.concatenate([moved[:, :cols - 128], tail], axis=1)

    def from_left(x, ghost):
        moved = pltpu.roll(x, 1, axis=1)
        if ghost is None:
            return moved
        head = jnp.where(lane128 == 0, ghost, moved[:, :128])
        return jnp.concatenate([head, moved[:, 128:]], axis=1)

    def new_pressure(p, k, u, below, v, left):
        q = p - COURANT * k * ((u - below) + (v - from_left(v, left)))
        a, b, c = pieces(q)
        return q + jnp.dot(mix[...], jnp.concatenate([a, b, a, b, c, a], axis=0), preferred_element_type=F32)

    def nest_u(s, i):
        n_u[i] = n_u[i] - COURANT * (n_p[s, i + 1] - n_p[s, i])

    def nest_v(s, i, t):
        p = n_p[s, i + 1]
        v = n_v[i] - COURANT * (from_right(p, edge[t, 0]) - p)
        n_v[i] = v
        return p, v

    def nest_row(s, i, t):
        nest_u(s, i + 1)

        @pl.when(first & (i == 0))
        def _():
            n_u[1] = b_row[...]
        p, v = nest_v(s, i, t)
        n_p[s + 1, i + 1] = new_pressure(p, n_k[i], n_u[i + 1], n_u[i], v, edge[t, 1])

    def above_nest(s):
        @pl.when(last)
        def _():
            n_p[s, 5] = a_row[...]

    def nest_first(s):
        above_nest(s)
        nest_u(s, 0)
        loop(0, 5, lambda i: nest_row(s, i, (i + 2) // RATIO))
        if s < 4:
            send(n_p.at[s + 1, 3], n_p.at[s + 1, 0], nm_send.at[s // 2, 0], nm_recv.at[s // 2, 0], me + 1, ~last)
            send(n_p.at[s + 1, 3], n_p.at[s + 1, 6], nm_send.at[s // 2, 1], nm_recv.at[s // 2, 1], me - 1, ~first)

    def nest_second(s):
        above_nest(s)
        nest_u(s, 1)

        @pl.when(first)
        def _():
            n_u[1] = b_row[...]

        def up(i):
            return remote(n_p.at[s + 1, i + 3], n_p.at[s + 1, i], nx_send.at[s // 2, 0, i], nx_recv.at[s // 2, 0, i], me + 1)

        def down(i):
            return remote(n_p.at[s + 1, i + 2], n_p.at[s + 1, i + 5], nx_send.at[s // 2, 1, i], nx_recv.at[s // 2, 1, i], me - 1)

        def row(r):
            nest_row(s, r + 1, 1)
            if s < 5:
                pl.when((r >= 1) & ~last)(lambda: up(jnp.maximum(r - 1, 0)).start())
                pl.when((r <= 1) & ~first)(lambda: down(jnp.minimum(r, 1)).start())
        loop(0, 3, row)
        if s < 5:
            for i in range(2):
                finish.append(lambda i=i: pl.when(~last)(up(i).wait_send))
                finish.append(lambda i=i: pl.when(~first)(down(i).wait_send))
            nest_v(s, 0, 0)
            nest_v(s, 4, 2)
            arrived(n_p.at[s, 0], nm_recv.at[s // 2, 0], ~first)
            arrived(n_p.at[s, 6], nm_recv.at[s // 2, 1], ~last)
            nest_u(s, 0)
            nest_u(s, 5)

    def nest_arrived(s):
        for i in range(2):
            arrived(n_p.at[s, i], nx_recv.at[s // 2 - 1, 0, i], ~first)
            arrived(n_p.at[s, 5 + i], nx_recv.at[s // 2 - 1, 1, i], ~last)

    def parent_substep(s):
        arrived(p_p.at[s, 0], px_recv.at[s, 0], ~first)
        arrived(p_p.at[s, 4], px_recv.at[s, 1], ~last)
        if s == 0:
            arrived(p_u.at[0], px_recv.at[0, 2], ~first)

        def parent_u(i):
            p_u[i] = p_u[i] - COURANT * (p_p[s, i + 1] - p_p[s, i])

            @pl.when((first & (i == 0)) | (last & (i == RATIO)))
            def _():
                p_u[i] = jnp.zeros((levels, cols), F32)
        parent_u(0)

        def row(r):
            parent_u(r + 1)
            p = p_p[s, r + 1]
            v = p_v[r] - COURANT * (from_right(p, None) - p)
            p_v[r] = v
            p_p[s + 1, r + 1] = new_pressure(p, p_k[r], p_u[r + 1], p_u[r], v, None)
        loop(0, RATIO, row)

    def owner_edges():
        for w in range(2):
            base = me + n * w
            for m in range(4):
                owner = base // RATIO + m
                slot = base % RATIO + 7 - RATIO * m
                cond = (slot >= 0) & (owner < owners)
                if w == 1:
                    cond = cond & (me < 8 * STRIDE)
                yield owner, cond, jnp.clip(slot, 0, 9), 4 * w + m

    def start_feedback(o):
        rows = n_p.at[3 * (o + 1)]
        a, b, c = pieces((rows[2] + rows[3]) + rows[4])
        mean = jnp.dot(jnp.concatenate([a, b, c], axis=0), fold[...], preferred_element_type=F32)
        f_one[o][0] = ((mean[:levels] + mean[levels:2 * levels]) + mean[2 * levels:]) * (1.0 / (RATIO * RATIO))

        def onward(i):
            b = i + 1
            return remote(f_one[o].at[0], f_one[o].at[b], f1_send.at[o, i], f1_recv.at[o], (me + STRIDE * b) % n), True
        send_each(7, onward)

    def pass_feedback(o):
        arrived(f_one[o].at[pl.ds(1, 7)], f1_recv.at[o])
        f_mid[o] = f_one[o][shift_b]
        for owner, cond, slot, here in owner_edges():
            @pl.when(cond & (owner == me))
            def _():
                f_two[o][slot] = f_mid[o]
            send(f_mid.at[o], f_two[o].at[slot], f2_send.at[o, here], f2_recv.at[o, slot], owner % n, cond & (owner != me))

    def take_feedback(o, source, target):
        def wait(k):
            base = own + k - 7
            arrived(f_two[o].at[k], f2_recv.at[o, k], (base >= 0) & (me < owners) & ((base + n) % n != me))
        loop(0, 10, wait)
        under = (lane >= y0) & (lane < y0 + win)

        def place(j):
            row = own + j
            value = f_two[o][j - shift_c + 7]
            value = pltpu.roll(jnp.concatenate([value, jnp.zeros((levels, cols - win), F32)], axis=1), y0, axis=1)
            inside = ((row >= x0) & (row < x0 + n)).astype(jnp.int32)
            target[j] = jnp.where(under & (jnp.broadcast_to(inside, (levels, cols)) > 0), value, source[j])
        loop(0, RATIO, place)

    for name in ("pp", "pv", "pu"):
        loads[name].wait()
    parent_rows = [p_p.at[s, pl.ds(1, 3)] for s in range(3)]
    start_ghosts(0, parent_rows[0], p_u.at[pl.ds(1, 3)])

    spot = lax.broadcasted_iota(jnp.int32, (cols, win), 0) - RATIO * lax.broadcasted_iota(jnp.int32, (cols, win), 1)
    fold[...] = jnp.where((spot >= 0) & (spot < RATIO), 1.0, 0.0).astype(BF16)
    block = lax.broadcasted_iota(jnp.int32, (levels, 6 * levels), 1)
    copies = (block % levels == lax.broadcasted_iota(jnp.int32, (levels, 6 * levels), 0)).astype(F32)
    wide = jnp.dot(MIXING * vert_ref[...], copies, precision=lax.Precision.HIGHEST, preferred_element_type=F32)
    m1, m2, m3 = (x.astype(F32) for x in pieces(wide))
    part = block // levels
    mix[...] = jnp.where(part >= 5, m3, jnp.where((part == 2) | (part == 3), m2, m1)).astype(BF16)

    loads["pk"].wait()
    pass_ghosts(0)
    parent_substep(0)
    start_ghosts(1, parent_rows[1], p_u.at[pl.ds(1, 3)])
    for name in ("np", "nu", "nv", "nk"):
        loads[name].wait()
    take_ghosts(0)
    for i in range(4):
        arrived(to_up[i][1], ni_recv.at[0, i], ~first)
        arrived(to_down[i][1], ni_recv.at[1, i], ~last)
    nest_first(0)
    nest_second(1)
    pass_ghosts(1)
    nest_arrived(2)
    nest_first(2)
    take_ghosts(1)
    nest_second(3)
    start_feedback(0)
    nest_arrived(4)
    nest_first(4)
    nest_second(5)
    start_feedback(1)
    outs = []

    def store(src, dst):
        outs.append(pltpu.make_async_copy(src, dst, out_sem.at[len(outs)]))
        outs[-1].start()
    store(n_p.at[6, pl.ds(2, 3)], p_out.at[1])
    store(n_u.at[pl.ds(2, 3)], u_out.at[1])
    store(n_v.at[pl.ds(1, 3)], v_out.at[1])
    pass_feedback(0)
    take_feedback(0, parent_rows[1], parent_rows[1])
    parent_exchange(1, parent_rows[1])
    pass_feedback(1)
    parent_substep(1)
    store(p_u.at[pl.ds(1, 3)], u_out.at[0])
    store(p_v, v_out.at[0])
    take_feedback(1, parent_rows[2], p_out.at[0])
    for wait in finish:
        wait()
    for copy in outs:
        copy.wait()


def put_out(p, u, v, p_out, u_out, v_out, sem):
    copies = [pltpu.make_async_copy(a, b, sem.at[i]) for i, (a, b) in enumerate(((p, p_out), (u, u_out), (v, v_out)))]
    for copy in copies:
        copy.start()
    for copy in copies:
        copy.wait()


def per_device(n, tiles, pressure, u_wind, v_wind, stiffness, vertical, nest_row0, nest_col0):
    fields = [jnp.transpose(x, (0, 2, 1, 3)) for x in (pressure, u_wind, v_wind, stiffness)]
    fields = [pltpu.with_memory_space_constraint(x, pltpu.HBM) for x in fields]
    _, rows, levels, cols = fields[0].shape
    win = cols // RATIO
    row = (levels, cols)
    owners = (LAST_X0 + n) // RATIO + 1
    a_count = owners - (1 + n) // RATIO
    b_count = (LAST_X0 - 1) // RATIO + 1
    vmem = lambda *shape: pltpu.VMEM(shape, F32)
    dma = lambda *shape: pltpu.SemaphoreType.DMA(shape)
    outs = pl.pallas_call(
        functools.partial(kernel, n, tiles),
        out_shape=[pltpu.VMEM((2, rows) + row, F32)] * 3,
        in_specs=[pl.BlockSpec(memory_space=pltpu.SMEM)] * 2
        + [pl.BlockSpec(memory_space=pltpu.VMEM)]
        + [pl.BlockSpec(memory_space=pl.ANY)] * 4,
        out_specs=[pl.BlockSpec(memory_space=pltpu.VMEM)] * 3,
        scratch_shapes=[
            vmem(7, 7, *row), vmem(6, *row), vmem(5, *row), vmem(5, *row),
            vmem(3, 5, *row), vmem(4, *row), vmem(3, *row), vmem(3, *row),
            vmem(OUTER, 8, 128), vmem(OUTER, 8, 128), vmem(OUTER, levels, win), vmem(OUTER, levels, win),
            vmem(OUTER, levels, win), vmem(*row), vmem(*row), vmem(3, 2, levels, 128),
            pltpu.VMEM((cols, win), BF16), pltpu.VMEM((levels, 6 * levels), BF16),
            *[vmem(8, 8, 128)] * 4,
            *[vmem(a_count, levels, win)] * 2, *[vmem(b_count, levels, win)] * 2,
            *[vmem(8, levels, win)] * 2, *[vmem(10, levels, win)] * 2,
            dma(8), dma(5), dma(2, 4), dma(2, 4), dma(2, 2, 2), dma(2, 2, 2), dma(2, 2), dma(2, 2), dma(2, 3), dma(2, 3),
            dma(OUTER, 12), dma(OUTER, 8), dma(OUTER, 7), dma(OUTER), dma(OUTER, 2), dma(OUTER, 2),
            dma(OUTER, 7), dma(OUTER), dma(OUTER, 8), dma(OUTER, 10),
        ],
        compiler_params=pltpu.CompilerParams(has_side_effects=True, vmem_limit_bytes=48 * 1024 * 1024),
        cost_estimate=pl.CostEstimate(flops=300_000_000, bytes_accessed=4_200_000, transcendentals=0),
    )(nest_row0, nest_col0, vertical, *fields)
    outs = pl.pallas_call(
        put_out,
        out_shape=[jax.ShapeDtypeStruct((2, rows) + row, F32)] * 3,
        in_specs=[pl.BlockSpec(memory_space=pltpu.VMEM)] * 3,
        out_specs=[pl.BlockSpec(memory_space=pl.ANY)] * 3,
        scratch_shapes=[dma(3)],
    )(*[pltpu.with_memory_space_constraint(x, pltpu.VMEM) for x in outs])
    return tuple(jnp.transpose(x, (0, 2, 1, 3)) for x in outs)


def solution(mesh):
    spec = P(None, None, ("grp", "tile"), None)
    tiles = mesh.shape["tile"]
    return jax.shard_map(
        functools.partial(per_device, mesh.shape["grp"] * tiles, tiles),
        mesh=mesh,
        in_specs=(spec, spec, spec, spec, P(), P(), P()),
        out_specs=(spec, spec, spec),
        check_vma=False,
    )
```

time: 80.4 us -> 81.9 us (1.019)
  the two profiles are of different devices: /device:TPU:8 before, /device:TPU:24 now
where the time goes in v2:
time: 81.9 us; the launch traced here: 81.7 us
  Pallas kernels  79.6 us (97%)
  local copies, waits for them, and re-layouts  1.39 us (2%)
    pallas_call x1, Pallas kernels, per_device(): pl.pallas_call(functools.partial(kernel, n, tiles), out_shape=[pltpu.VMEM...  78.4 us

profile of v2, /device:TPU:24, one launch (start us, length us, event | category | flops | bytes accessed | tf_op | source)
XLA Modules:
  0.0 81.7 jit_solution(16936597592188330245)
XLA Ops:
  0.6 0.0 copy-start.1
  0.6 0.0 copy-start.2
  0.7 0.7 copy-done.1
  1.3 0.0 copy-done.2
  1.3 0.0 copy-start
  1.3 0.7 copy-done
  2.0 78.4 %shard_map.94 = (f32[2,3,32,768]{3,2,1,0:T(8,128)S(1)}, f32[2,3,32,768]{3,2,1,0:T(8,128)S(1)}, f32[2,3,32,768]{3,2,1,0:T(8,128)S(1)}) custom-call(s32[60]{0:T(128)S(1)} %copy-done.2, s32[511]{0:T(512)S(1)} %copy-done.1, f32[32,32]{1,0:T(8,128)S(1)} %copy-done, f32[2,3,32,768]{3,2,1,0:T(8,128)} %bitcast.7, f32[2,3,32,768]{3,2,1,0:T(8,128)} %bitcast.8, ...), custom_call_target="tpu_custom_call" | custom-call | flops 300000000 | bytes 4200000 | tf_op jit(solution)/shard_map/pallas_call | solution.py:444
  80.5 1.2 %shard_map.95 = (f32[2,3,32,768]{3,2,1,0:T(8,128)}, f32[2,3,32,768]{3,2,1,0:T(8,128)}, f32[2,3,32,768]{3,2,1,0:T(8,128)}) custom-call(f32[2,3,32,768]{3,2,1,0:T(8,128)S(1)} %get-tuple-element.9.p, f32[2,3,32,768]{3,2,1,0:T(8,128)S(1)} %get-tuple-element.10.u, f32[2,3,32,768]{3,2,1,0:T(8,128)S(1)} %get-tuple-element.11.v), custom_call_target="tpu_custom_call" | custom-call | tf_op jit(solution)/shard_map/pallas_call | solution.py:467
Async XLA Ops:
  0.6 0.7 copy-start.1
  0.6 0.7 copy-start.2
  1.3 0.7 copy-start

commit v3 on v0

v3 whole, which is shorter than its diff:
```python
import functools

import jax
import jax.numpy as jnp
from jax import lax
from jax.experimental import pallas as pl
from jax.experimental.pallas import tpu as pltpu
from jax.sharding import PartitionSpec as P

RATIO = 3
OUTER = 2
BLOCKS = 3
COURANT = 0.3
MIXING = 0.15
LAST_X0 = 60
GROUP = 6
MESH = pl.DeviceIdType.MESH
F32 = jnp.float32
BF16 = jnp.bfloat16


def pieces(x):
    a = x.astype(BF16)
    rest = x - a.astype(F32)
    b = rest.astype(BF16)
    c = (rest - b.astype(F32)).astype(BF16)
    return a, b, c


def kernel(
    n, tiles, lead,
    row0_in, col0_in, vert_in, p_in, u_in, v_in, k_in,
    p_out, u_out, v_out,
    n_p, n_u, n_v, n_k, p_p, p_u, p_v, p_k,
    g_send, g_recv, a_send, a_recv, b_send, b_recv, a_row, b_row, edge, f_send, f_recv, fold, mix,
    row0_ref, col0_ref, vert_ref,
    in_sem, out_sem, ni_send, ni_recv, nx_send, nx_recv, nm_send, nm_recv, px_send, px_recv,
    gs_send, gs_recv, e_send, a_sems, b_sems, f_sends, f_recvs,
):
    levels, cols = n_k.shape[1], n_k.shape[2]
    win = cols // RATIO
    me = lax.axis_index("grp") * tiles + lax.axis_index("tile")
    first, last = me == 0, me == n - 1
    own = RATIO * me
    finish = []

    def dev(d):
        d = d + 0 * me
        return (d // tiles, d % tiles)

    def remote(src, dst, s_sem, r_sem, to):
        return pltpu.make_async_remote_copy(
            src_ref=src, dst_ref=dst, send_sem=s_sem, recv_sem=r_sem, device_id=dev(to), device_id_type=MESH
        )

    def loop(low, high, body):
        lax.fori_loop(low, high, lambda i, _: (body(i), 0)[1], 0)

    def rows_of(count, body):
        for i in range(count):
            body(i)

    def arrived(ref, sem, cond=True):
        @pl.when(cond)
        def _():
            pltpu.make_async_copy(ref, ref, sem).wait()

    small = [
        pltpu.make_async_copy(src, dst, in_sem.at[8 + i])
        for i, (src, dst) in enumerate(((row0_in, row0_ref), (col0_in, col0_ref), (vert_in, vert_ref)))
    ]
    for copy in small:
        copy.start()
    loads = {}
    for at, (name, src, g, dst) in enumerate((
        ("pp", p_in, 0, p_p.at[0, pl.ds(1, 3)]), ("pv", v_in, 0, p_v), ("pu", u_in, 0, p_u.at[pl.ds(1, 3)]),
        ("np", p_in, 1, n_p.at[0, pl.ds(2, 3)]), ("nu", u_in, 1, n_u.at[pl.ds(2, 3)]),
        ("nv", v_in, 1, n_v.at[pl.ds(1, 3)]), ("nk", k_in, 1, n_k.at[pl.ds(1, 3)]), ("pk", k_in, 0, p_k),
    )):
        loads[name] = pltpu.make_async_copy(src.at[g], dst, in_sem.at[at])
        loads[name].start()

    ghosts_from, ghosts_to = g_recv.shape[1], GROUP + 4
    backs_to, backs_from = f_sends.shape[1], f_recv.shape[1]

    def ghost_to(k):
        d = own - lead + k - GROUP
        return d, (d >= 0) & (d < n), me - (d + lead + 2) // RATIO + 1

    def ghost_from(i):
        e = (me + lead + 2) // RATIO - 1 + i
        return e, (e >= 0) & (RATIO * e <= lead + me + GROUP)

    def back_to(i):
        e = (me + lead) // RATIO + i
        return e, RATIO * e < lead + me + GROUP, jnp.clip(me + lead - RATIO * e + GROUP - 1, 0, backs_from - 1)

    def back_from(k):
        d = own - lead + k - GROUP + 1
        return d, (d >= 0) & (d < n)

    a_from = tuple(range((lead + n) // RATIO, (lead + n + GROUP - 1) // RATIO + 1))
    b_from = tuple(range((lead - 1) // RATIO, (lead + GROUP - 2) // RATIO + 1))

    bar = pltpu.get_barrier_semaphore()
    count = jnp.where(first | last, 1, 2)

    def hello(d, cond):
        @pl.when(cond)
        def _():
            pl.semaphore_signal(bar, inc=1, device_id=dev(d), device_id_type=MESH)
    hello(me + 1, ~last)
    hello(me - 1, ~first)
    for i in range(ghosts_from):
        e, cond = ghost_from(i)
        hello(e, cond & (e != me))
    for k in range(ghosts_to):
        d, cond, _ = ghost_to(k)
        count = count + jnp.where(cond & (d != me), 1, 0)
    for k in range(backs_from):
        d, cond = back_from(k)
        hello(d, cond & (d != me))
    for i in range(backs_to):
        e, cond, _ = back_to(i)
        count = count + jnp.where(cond & (e != me), 1, 0)
    for e in a_from:
        hello(e, last)
        count = count + jnp.where(me == e, 1, 0)
    for e in b_from:
        if e > 0:
            hello(e, first)
            count = count + jnp.where(me == e, 1, 0)
    pl.semaphore_wait(bar, count)

    def parent_copies(s, rows):
        return (
            (remote(rows.at[2], p_p.at[s, 0], px_send.at[s, 0], px_recv.at[s, 0], me + 1), ~last),
            (remote(rows.at[0], p_p.at[s, 4], px_send.at[s, 1], px_recv.at[s, 1], me - 1), ~first),
        )

    to_up = (
        (p_in.at[1, 2], n_p.at[0, 1], nx_send.at[0, 0, 1], nx_recv.at[0, 0, 1]),
        (p_in.at[1, 1], n_p.at[0, 0], nx_send.at[0, 0, 0], nx_recv.at[0, 0, 0]),
        (u_in.at[1, pl.ds(1, 2)], n_u.at[pl.ds(0, 2)], ni_send.at[0, 0], ni_recv.at[0, 0]),
        (v_in.at[1, 2], n_v.at[0], ni_send.at[0, 1], ni_recv.at[0, 1]),
        (k_in.at[1, 2], n_k.at[0], ni_send.at[0, 2], ni_recv.at[0, 2]),
        (u_in.at[0, 2], p_u.at[0], px_send.at[0, 2], px_recv.at[0, 2]),
    )
    to_down = (
        (p_in.at[1, 0], n_p.at[0, 5], nx_send.at[0, 1, 0], nx_recv.at[0, 1, 0]),
        (p_in.at[1, 1], n_p.at[0, 6], nx_send.at[0, 1, 1], nx_recv.at[0, 1, 1]),
        (u_in.at[1, 0], n_u.at[5], ni_send.at[1, 0], ni_recv.at[1, 0]),
        (v_in.at[1, 0], n_v.at[4], ni_send.at[1, 1], ni_recv.at[1, 1]),
        (k_in.at[1, 0], n_k.at[4], ni_send.at[1, 2], ni_recv.at[1, 2]),
    )
    for i in range(6):
        for group, to, cond in ((to_up, me + 1, ~last), (to_down, me - 1, ~first)):
            if i < len(group):
                copy = remote(*group[i], to)
                pl.when(cond)(copy.start)
                finish.append(lambda copy=copy, cond=cond: pl.when(cond)(copy.wait_send))
    for copy, cond in parent_copies(0, p_in.at[0]):
        pl.when(cond)(copy.start)

    for copy in small:
        copy.wait()
    x0, y0 = row0_ref[0], col0_ref[0]
    rest = x0 - lead
    lane = lax.broadcasted_iota(jnp.int32, (levels, cols), 1)
    lane128 = lax.broadcasted_iota(jnp.int32, (levels, 128), 1)
    level128 = lax.broadcasted_iota(jnp.int32, (levels, 128), 0)
    row8 = lax.broadcasted_iota(jnp.int32, (8, 128), 0)

    def ghost_copy(o, k):
        d, cond, slot = ghost_to(k)
        return remote(g_send.at[o], g_recv.at[o, slot], gs_send.at[o, k], gs_recv.at[o, slot], d), cond & (d != me)

    def row_copies(o):
        for i, e in enumerate(a_from):
            yield remote(a_send.at[o], a_recv.at[o, i], e_send.at[o, 0], a_sems.at[o, i], n - 1), me == e
        for i, e in enumerate(b_from):
            if e > 0:
                yield remote(b_send.at[o], b_recv.at[o, i], e_send.at[o, 1], b_sems.at[o, i], 0), me == e

    def start_ghosts(o):
        pp, pu = p_p.at[o, pl.ds(1, 3)], p_u.at[pl.ds(1, 3)]

        def gather(j, total):
            right = jnp.sum(jnp.where(lane == y0 + win, pp[j], 0.0), axis=1, keepdims=True)
            left = jnp.sum(jnp.where(lane == y0 - 1, p_v[j], 0.0), axis=1, keepdims=True)
            both = jnp.where(level128 == lane128, right, 0.0) + jnp.where(level128 == lane128 - levels, left, 0.0)
            return jnp.where(row8 == j, jnp.sum(both, axis=0, keepdims=True), total)
        g_send[o] = lax.fori_loop(0, RATIO, gather, jnp.zeros((8, 128), F32))

        def column(k):
            d, cond, slot = ghost_to(k)

            @pl.when(cond & (d == me))
            def _():
                g_recv[o, slot] = g_send[o]
            copy, cond = ghost_copy(o, k)
            pl.when(cond)(copy.start)
        loop(0, ghosts_to, column)

        def pick_row(field, target):
            out = jnp.zeros((levels, cols), F32)
            for j in range(RATIO):
                out = jnp.where(target == own + j, field[j], out)
            return pltpu.roll(out, cols - y0, axis=1)[:, :win]

        @pl.when((me >= a_from[0]) & (me <= a_from[-1]))
        def _():
            a_send[o] = pick_row(pp, x0 + n)

        @pl.when((me >= b_from[0]) & (me <= b_from[-1]))
        def _():
            b_send[o] = pick_row(pu, x0 - 1)
        if b_from[0] == 0:
            @pl.when(first)
            def _():
                b_recv[o, 0] = b_send[o]
        for copy, cond in row_copies(o):
            pl.when(cond)(copy.start)

    def end_ghosts(o):
        def column(k):
            copy, cond = ghost_copy(o, k)
            pl.when(cond)(copy.wait_send)
        loop(0, ghosts_to, column)
        for copy, cond in row_copies(o):
            pl.when(cond)(copy.wait_send)

    def take_ghosts(o):
        for i in range(ghosts_from):
            e, cond = ghost_from(i)
            arrived(g_recv.at[o, i], gs_recv.at[o, i], cond & (e != me))
        for t in range(3):
            place = (me + lead + 2) % RATIO + rest + t
            row = jnp.zeros((1, 128), F32)
            for i in range(ghosts_from):
                row = row + jnp.sum(jnp.where(row8 == place - RATIO * i, g_recv[o, i], 0.0), axis=0, keepdims=True)
            right = jnp.sum(jnp.where(level128 == lane128, row, 0.0), axis=1, keepdims=True)
            left = jnp.sum(jnp.where(level128 == lane128 - levels, row, 0.0), axis=1, keepdims=True)
            edge[o, t, 0] = jnp.broadcast_to(right, (levels, 128))
            edge[o, t, 1] = jnp.broadcast_to(left, (levels, 128))

        @pl.when(first | last)
        def _():
            a = b = jnp.zeros((levels, win), F32)
            for i, e in enumerate(a_from):
                arrived(a_recv.at[o, i], a_sems.at[o, i], last)
                a = jnp.where((x0 + n >= RATIO * e) & (x0 + n < RATIO * (e + 1)), a_recv[o, i], a)
            for i, e in enumerate(b_from):
                if e > 0:
                    arrived(b_recv.at[o, i], b_sems.at[o, i], first)
                b = jnp.where((x0 - 1 >= RATIO * e) & (x0 - 1 < RATIO * (e + 1)), b_recv[o, i], b)
            x = jnp.where(jnp.broadcast_to(last.astype(jnp.int32), a.shape) > 0, a, b)
            wide = lax.dot_general(
                jnp.concatenate(pieces(x), axis=0), fold[...], (((1,), (1,)), ((), ())), preferred_element_type=F32
            )
            wide = (wide[:levels] + wide[levels:2 * levels]) + wide[2 * levels:]
            a_row[o] = wide
            b_row[o] = wide

    def from_right(x, ghost):
        moved = pltpu.roll(x, cols - 1, axis=1)
        if ghost is None:
            return moved
        tail = jnp.where(lane128 == 127, ghost, moved[:, cols - 128:])
        return jnp.concatenate([moved[:, :cols - 128], tail], axis=1)

    def from_left(x, ghost):
        moved = pltpu.roll(x, 1, axis=1)
        if ghost is None:
            return moved
        head = jnp.where(lane128 == 0, ghost, moved[:, :128])
        return jnp.concatenate([head, moved[:, 128:]], axis=1)

    def new_pressure(p, k, u, below, v, left):
        q = p - COURANT * k * ((u - below) + (v - from_left(v, left)))
        a = q.astype(BF16)
        b = (q - a.astype(F32)).astype(BF16)
        return q + jnp.dot(mix[...], jnp.concatenate([a, b, a], axis=0), preferred_element_type=F32)

    def nest_u(s, i):
        n_u[i] = n_u[i] - COURANT * (n_p[s, i + 1] - n_p[s, i])

    def nest_v(s, o, i, t):
        p = n_p[s, i + 1]
        v = n_v[i] - COURANT * (from_right(p, edge[o, t, 0]) - p)
        n_v[i] = v
        return p, v

    def below_nest(o):
        @pl.when(first)
        def _():
            n_u[1] = b_row[o]

    def above_nest(s, o):
        @pl.when(last)
        def _():
            n_p[s, 5] = a_row[o]

    def nest_row(s, o, i, t):
        p, v = nest_v(s, o, i, t)
        n_p[s + 1, i + 1] = new_pressure(p, n_k[i], n_u[i + 1], n_u[i], v, edge[o, t, 1])

    def middle_copies(blk):
        s = 2 * blk + 1
        return (
            (remote(n_p.at[s, 3], n_p.at[s, 0], nm_send.at[blk, 0], nm_recv.at[blk, 0], me + 1), ~last),
            (remote(n_p.at[s, 3], n_p.at[s, 6], nm_send.at[blk, 1], nm_recv.at[blk, 1], me - 1), ~first),
        )

    def end_copies(blk):
        s, nxt = 2 * blk + 2, blk + 1
        up = [remote(n_p.at[s, i + 3], n_p.at[s, i], nx_send.at[nxt, 0, i], nx_recv.at[nxt, 0, i], me + 1) for i in range(2)]
        down = [remote(n_p.at[s, i + 2], n_p.at[s, i + 5], nx_send.at[nxt, 1, i], nx_recv.at[nxt, 1, i], me - 1) for i in range(2)]
        return up, down

    def nest_block(blk):
        s = 2 * blk
        before, after = blk // 2, (blk + 1) // 2
        for i in range(2):
            arrived(n_p.at[s, i], nx_recv.at[blk, 0, i], ~first)
            arrived(n_p.at[s, 5 + i], nx_recv.at[blk, 1, i], ~last)

        @pl.when(blk > 0)
        def _():
            arrived(n_p.at[s - 1, 0], nm_recv.at[blk - 1, 0], ~first)
            arrived(n_p.at[s - 1, 6], nm_recv.at[blk - 1, 1], ~last)
            nest_u(s - 1, 0)
            nest_u(s - 1, 5)
        pl.when(blk < 2)(lambda: take_ghosts(blk))

        above_nest(s, before)
        for i in range(6):
            nest_u(s, i)
        below_nest(before)
        for i in (2, 1, 3, 4, 0):
            nest_row(s, before, i, (i + 2) // RATIO)

        @pl.when(blk < BLOCKS - 1)
        def _():
            for copy, cond in middle_copies(blk):
                pl.when(cond)(copy.start)

        above_nest(s + 1, after)
        for i in range(1, 5):
            nest_u(s + 1, i)
        below_nest(after)
        up, down = end_copies(blk)
        more = blk < BLOCKS - 1
        nest_row(s + 1, after, 2, 1)
        pl.when(more & ~last)(up[0].start)
        pl.when(more & ~first)(down[1].start)
        nest_row(s + 1, after, 3, 1)
        pl.when(more & ~last)(up[1].start)
        nest_row(s + 1, after, 1, 1)
        pl.when(more & ~first)(down[0].start)

        @pl.when(more)
        def _():
            nest_v(s + 1, after, 0, 0)
            nest_v(s + 1, after, 4, 2)

    def parent_substep(s):
        arrived(p_p.at[s, 0], px_recv.at[s, 0], ~first)
        arrived(p_p.at[s, 4], px_recv.at[s, 1], ~last)
        for i in range(4):
            p_u[i] = p_u[i] - COURANT * (p_p[s, i + 1] - p_p[s, i])

        @pl.when(first)
        def _():
            p_u[0] = jnp.zeros((levels, cols), F32)

        @pl.when(last)
        def _():
            p_u[3] = jnp.zeros((levels, cols), F32)

        def row(r):
            p = p_p[s, r + 1]
            v = p_v[r] - COURANT * (from_right(p, None) - p)
            p_v[r] = v
            p_p[s + 1, r + 1] = new_pressure(p, p_k[r], p_u[r + 1], p_u[r], v, None)
        rows_of(RATIO, row)

    def back_copy(o, i):
        e, cond, slot = back_to(i)
        return remote(f_send.at[o], f_recv.at[o, slot], f_sends.at[o, i], f_recvs.at[o, slot], e), cond & (e != me)

    def start_feedback(o):
        rows = n_p.at[3 * (o + 1)]
        stack = jnp.concatenate(pieces((rows[2] + rows[3]) + rows[4]), axis=0)
        mean = jnp.dot(stack, fold[...], preferred_element_type=F32)
        f_send[o] = ((mean[:levels] + mean[levels:2 * levels]) + mean[2 * levels:]) * (1.0 / (RATIO * RATIO))
        for i in range(backs_to):
            e, cond, slot = back_to(i)

            @pl.when(cond & (e == me))
            def _():
                f_recv[o, slot] = f_send[o]
            copy, cond = back_copy(o, i)
            pl.when(cond)(copy.start)

    def take_feedback(o, target):
        for k in range(backs_from):
            d, cond = back_from(k)
            arrived(f_recv.at[o, k], f_recvs.at[o, k], cond & (d != me))
        under = (lane >= y0) & (lane < y0 + win)

        def place(j):
            row = own + j
            value = f_recv[o, j + GROUP - 1]
            for i in range(1, GROUP):
                value = jnp.where(rest == i, f_recv[o, j + GROUP - 1 - i], value)
            value = pltpu.roll(jnp.concatenate([value, jnp.zeros((levels, cols - win), F32)], axis=1), y0, axis=1)
            inside = ((row >= x0) & (row < x0 + n)).astype(jnp.int32)
            target[j] = jnp.where(under & (jnp.broadcast_to(inside, (levels, cols)) > 0), value, p_p[o + 1, j + 1])
        loop(0, RATIO, place)

    for name in ("pp", "pv", "pu"):
        loads[name].wait()
    spot = lax.broadcasted_iota(jnp.int32, (cols, win), 0) - RATIO * lax.broadcasted_iota(jnp.int32, (cols, win), 1)

    def stores():
        pairs = (
            (n_p.at[6, pl.ds(2, 3)], p_out.at[1]), (n_u.at[pl.ds(2, 3)], u_out.at[1]), (n_v.at[pl.ds(1, 3)], v_out.at[1]),
            (p_u.at[pl.ds(1, 3)], u_out.at[0]), (p_v, v_out.at[0]),
        )
        return [pltpu.make_async_copy(src, dst, out_sem.at[i]) for i, (src, dst) in enumerate(pairs)]

    def turn(it):
        pl.when(it < OUTER)(lambda: start_ghosts(it))

        @pl.when(it == 0)
        def _():
            fold[...] = jnp.where((spot >= 0) & (spot < RATIO), 1.0, 0.0).astype(BF16)
            block = lax.broadcasted_iota(jnp.int32, (levels, 3 * levels), 1)
            copies = (block % levels == lax.broadcasted_iota(jnp.int32, (levels, 3 * levels), 0)).astype(F32)
            wide = jnp.dot(MIXING * vert_ref[...], copies, precision=lax.Precision.HIGHEST, preferred_element_type=F32)
            m1, m2, _ = (x.astype(F32) for x in pieces(wide))
            mix[...] = jnp.where(block >= 2 * levels, m2, m1).astype(BF16)
            for name in ("np", "nu", "nv", "nk", "pk"):
                loads[name].wait()
            for i in range(3):
                arrived(to_up[i + 2][1], ni_recv.at[0, i], ~first)
                arrived(to_down[i + 2][1], ni_recv.at[1, i], ~last)
            arrived(p_u.at[0], px_recv.at[0, 2], ~first)
        nest_block(it)
        pl.when(it > 0)(lambda: start_feedback(it - 1))

        @pl.when(it == 2)
        def _():
            take_feedback(0, p_p.at[1, pl.ds(1, 3)])
            for copy, cond in parent_copies(1, p_p.at[1, pl.ds(1, 3)]):
                pl.when(cond)(copy.start)
            for copy in stores()[:3]:
                copy.start()
        pl.when(it != 1)(lambda: parent_substep(it // 2))
    loop(0, BLOCKS, turn)
    outs = stores()
    for copy in outs[3:]:
        copy.start()
    take_feedback(1, p_out.at[0])

    for o in range(OUTER):
        end_ghosts(o)
        for i in range(backs_to):
            copy, cond = back_copy(o, i)
            pl.when(cond)(copy.wait_send)
    for blk in range(BLOCKS - 1):
        for copy, cond in middle_copies(blk):
            pl.when(cond)(copy.wait_send)
        up, down = end_copies(blk)
        for i in range(2):
            pl.when(~last)(up[i].wait_send)
            pl.when(~first)(down[i].wait_send)
    for s, rows in ((0, p_in.at[0]), (1, p_p.at[1, pl.ds(1, 3)])):
        for copy, cond in parent_copies(s, rows):
            pl.when(cond)(copy.wait_send)
    for wait in finish:
        wait()
    for copy in outs:
        copy.wait()


def put_out(p, u, v, p_out, u_out, v_out, sem):
    copies = [pltpu.make_async_copy(a, b, sem.at[i]) for i, (a, b) in enumerate(((p, p_out), (u, u_out), (v, v_out)))]
    for copy in copies:
        copy.start()
    for copy in copies:
        copy.wait()


def per_device(n, tiles, pressure, u_wind, v_wind, stiffness, vertical, nest_row0, nest_col0):
    fields = [jnp.transpose(x, (0, 2, 1, 3)) for x in (pressure, u_wind, v_wind, stiffness)]
    operands = [pltpu.with_memory_space_constraint(x, pltpu.HBM) for x in (nest_row0, nest_col0, vertical, *fields)]
    _, rows, levels, cols = fields[0].shape
    win = cols // RATIO
    row = (levels, cols)
    vmem = lambda *shape: pltpu.VMEM(shape, F32)
    dma = lambda *shape: pltpu.SemaphoreType.DMA(shape)

    owners = lambda rows, at: (at + rows - 1) // RATIO - at // RATIO + 1

    def most(rows):
        return max(owners(rows, at) for at in range(RATIO))

    def call(lead):
        return pl.pallas_call(
            functools.partial(kernel, n, tiles, lead),
            out_shape=[pltpu.VMEM((2, rows) + row, F32)] * 3,
            in_specs=[pl.BlockSpec(memory_space=pl.ANY)] * 7,
            out_specs=[pl.BlockSpec(memory_space=pltpu.VMEM)] * 3,
            scratch_shapes=[
                vmem(7, 7, *row), vmem(6, *row), vmem(5, *row), vmem(5, *row),
                vmem(3, 5, *row), vmem(4, *row), vmem(3, *row), vmem(3, *row),
                vmem(OUTER, 8, 128), vmem(OUTER, most(GROUP + 2), 8, 128), vmem(OUTER, levels, win), vmem(OUTER, most(GROUP), levels, win),
                vmem(OUTER, levels, win), vmem(OUTER, most(GROUP), levels, win), vmem(OUTER, *row), vmem(OUTER, *row),
                vmem(OUTER, 3, 2, levels, 128), vmem(OUTER, levels, win), vmem(OUTER, GROUP + 2, levels, win),
                pltpu.VMEM((cols, win), BF16), pltpu.VMEM((levels, 3 * levels), BF16),
                pltpu.SMEM(nest_row0.shape, jnp.int32), pltpu.SMEM(nest_col0.shape, jnp.int32), vmem(*vertical.shape),
                dma(11), dma(5), dma(2, 3), dma(2, 3), dma(3, 2, 2), dma(3, 2, 2), dma(2, 2), dma(2, 2), dma(2, 3), dma(2, 3),
                dma(OUTER, GROUP + 4), dma(OUTER, most(GROUP + 2)), dma(OUTER, 2), dma(OUTER, most(GROUP)), dma(OUTER, most(GROUP)),
                dma(OUTER, most(GROUP)), dma(OUTER, GROUP + 2),
            ],
            compiler_params=pltpu.CompilerParams(
                collective_id=lead // GROUP, has_side_effects=True, vmem_limit_bytes=48 * 1024 * 1024
            ),
            cost_estimate=pl.CostEstimate(flops=300_000_000, bytes_accessed=4_200_000, transcendentals=0),
        )
    branches = [lambda *args, lead=lead: tuple(call(lead)(*args)) for lead in range(1, LAST_X0 + 1, GROUP)]
    outs = lax.switch((nest_row0[0] - 1) // GROUP, branches, *operands)
    outs = pl.pallas_call(
        put_out,
        out_shape=[jax.ShapeDtypeStruct((2, rows) + row, F32)] * 3,
        in_specs=[pl.BlockSpec(memory_space=pltpu.VMEM)] * 3,
        out_specs=[pl.BlockSpec(memory_space=pl.ANY)] * 3,
        scratch_shapes=[dma(3)],
    )(*[pltpu.with_memory_space_constraint(x, pltpu.VMEM) for x in outs])
    return tuple(jnp.transpose(x, (0, 2, 1, 3)) for x in outs)


def solution(mesh):
    spec = P(None, None, ("grp", "tile"), None)
    tiles = mesh.shape["tile"]
    return jax.shard_map(
        functools.partial(per_device, mesh.shape["grp"] * tiles, tiles),
        mesh=mesh,
        in_specs=(spec, spec, spec, spec, P(), P(), P()),
        out_specs=(spec, spec, spec),
        check_vma=False,
    )
```

time: 749 us -> 51 us (0.07)
  waiting for transfers between devices: 624 us -> 0 us
  Pallas kernels: 0 us -> 48.7 us
  starting transfers between devices: 40.4 us -> 0 us
  local copies, waits for them, and re-layouts: 31.3 us -> 0 us
  between operations: 20.5 us -> 1.55 us
  matrix products: 17.3 us -> 0 us
  other arithmetic: 14.1 us -> 0 us
    psum x4 -> x0, waiting for transfers between devices: 548 us -> none  [the longest x2 276 us: per_device(): lax.psum((row_p, row_u, col_p, col_v), ('grp', 'tile'))]
    ppermute x16 -> x0, waiting for transfers between devices: 75.5 us -> none  [passed_along(): lax.ppermute(value, axis, [(source, source + steps) for source in range(i...]
    pallas_call x0 -> x2, Pallas kernels: none -> 48.7 us  [the longest x1 47.5 us: per_device(): call(lead)(*args)]
    ppermute x16 -> x0, starting transfers between devices: 40.2 us -> none  [passed_along(): lax.ppermute(value, axis, [(source, source + steps) for source in range(i...]
    dot_general x14 -> x0, matrix products: 17.3 us -> none  [the longest x2 7.27 us: per_device(): jnp.einsum('ri,lrc->lic', selector, window, precision=lax.Precision.HIGHEST)]
    slice x46 -> x0, local copies, waits for them, and re-layouts: 8.01 us -> none  [the longest x8 1.8 us: substep(): p_rt = jnp.concatenate([p_field[:, :, 1:], right], axis=2)]
  transfers between devices with their start and end apart: 20 -> 0, of which waited for: 17 -> 0; matrix products, arithmetic and copies ran while one was open for 3% -> 0% of each run, Pallas kernels for 0% -> 0%
where the time goes in v3:
time: 51 us; the launch traced here: 50.8 us
  Pallas kernels  48.7 us (95%)
  between operations  1.55 us (3%)
  loops' own time  0.61 us (1%)
    pallas_call x1, Pallas kernels, per_device(): call(lead)(*args)  47.5 us
    pallas_call x1, Pallas kernels, per_device(): pl.pallas_call(put_out, out_shape=[jax.ShapeDtypeStruct((2, rows) + row,...  1.23 us

profile of v3, /device:TPU:8, one launch (start us, length us, event | category | flops | bytes accessed | tf_op | source)
XLA Modules:
  0.0 50.8 jit_solution(10095376489088172813)
XLA Ops:
  1.3 48.1 %conditional.1 = ((f32[2,3,32,768]{3,2,1,0:T(8,128)S(1)}, f32[2,3,32,768]{3,2,1,0:T(8,128)S(1)}, f32[2,3,32,768]{3,2,1,0:T(8,128)S(1)})) conditional(s32[]{:T(128)} %clamp.3, (s32[60]{0:T(128)}, s32[511]{0:T(512)}, f32[32,32]{1,0:T(8,128)}, f32[2,3,32,768]{3,2,1,0:T(8,128)}, f32[2,3,32,768]{3,2,1,0:T(8,128)}, ...), branch_computations={%region_0.1_spmd, %region_1.2_spmd, %region_2.3_spmd, %region_3.4_... | conditional | flops 300000000 | bytes 4200008 | solution.py:534
  1.3 47.5 %branch_1_fun.1 = (f32[2,3,32,768]{3,2,1,0:T(8,128)S(1)}, f32[2,3,32,768]{3,2,1,0:T(8,128)S(1)}, f32[2,3,32,768]{3,2,1,0:T(8,128)S(1)}) custom-call(s32[60]{0:T(128)} %get-tuple-element.147.row0_in, s32[511]{0:T(512)} %get-tuple-element.148.col0_in, f32[32,32]{1,0:T(8,128)} %get-tuple-element.149.vert_in, f32[2,3,32,768]{3,2,1,0:T(8,128)} %get-tuple-element.150.p_in, ...), custom_call_target="tpu_custom_call" | custom-call | flops 300000000 | bytes 4200000 | tf_op jit(solution)/shard_map/cond/branch_1_fun/pallas_call | solution.py:533
  49.4 1.2 %shard_map.94 = (f32[2,3,32,768]{3,2,1,0:T(8,128)}, f32[2,3,32,768]{3,2,1,0:T(8,128)}, f32[2,3,32,768]{3,2,1,0:T(8,128)}) custom-call(f32[2,3,32,768]{3,2,1,0:T(8,128)S(1)} %get-tuple-element.219.p, f32[2,3,32,768]{3,2,1,0:T(8,128)S(1)} %get-tuple-element.220.u, f32[2,3,32,768]{3,2,1,0:T(8,128)S(1)} %get-tuple-element.221.v), custom_call_target="tpu_custom_call" | custom-call | tf_op jit(solution)/shard_map/pallas_call | solution.py:535

commit v4 on v3

--- a/solution.py
+++ b/solution.py
@@ -132,6 +132,9 @@
             count = count + jnp.where(me == e, 1, 0)
     pl.semaphore_wait(bar, count)
 
+    def parent_u_copy():
+        return remote(u_in.at[0, 2], p_u.at[0], px_send.at[0, 2], px_recv.at[0, 2], me + 1)
+
     def parent_copies(s, rows):
         return (
             (remote(rows.at[2], p_p.at[s, 0], px_send.at[s, 0], px_recv.at[s, 0], me + 1), ~last),
@@ -144,7 +147,6 @@
         (u_in.at[1, pl.ds(1, 2)], n_u.at[pl.ds(0, 2)], ni_send.at[0, 0], ni_recv.at[0, 0]),
         (v_in.at[1, 2], n_v.at[0], ni_send.at[0, 1], ni_recv.at[0, 1]),
         (k_in.at[1, 2], n_k.at[0], ni_send.at[0, 2], ni_recv.at[0, 2]),
-        (u_in.at[0, 2], p_u.at[0], px_send.at[0, 2], px_recv.at[0, 2]),
     )
     to_down = (
         (p_in.at[1, 0], n_p.at[0, 5], nx_send.at[0, 1, 0], nx_recv.at[0, 1, 0]),
@@ -153,14 +155,12 @@
         (v_in.at[1, 0], n_v.at[4], ni_send.at[1, 1], ni_recv.at[1, 1]),
         (k_in.at[1, 0], n_k.at[4], ni_send.at[1, 2], ni_recv.at[1, 2]),
     )
-    for i in range(6):
+    for i in range(5):
         for group, to, cond in ((to_up, me + 1, ~last), (to_down, me - 1, ~first)):
             if i < len(group):
                 copy = remote(*group[i], to)
                 pl.when(cond)(copy.start)
                 finish.append(lambda copy=copy, cond=cond: pl.when(cond)(copy.wait_send))
-    for copy, cond in parent_copies(0, p_in.at[0]):
-        pl.when(cond)(copy.start)
 
     for copy in small:
         copy.wait()
@@ -321,9 +321,18 @@
     def nest_block(blk):
         s = 2 * blk
         before, after = blk // 2, (blk + 1) // 2
-        for i in range(2):
-            arrived(n_p.at[s, i], nx_recv.at[blk, 0, i], ~first)
-            arrived(n_p.at[s, 5 + i], nx_recv.at[blk, 1, i], ~last)
+        more = blk < BLOCKS - 1
+        up, down = end_copies(blk)
+
+        pl.when(blk == 0)(lambda: take_ghosts(0))
+        for i in (2, 3):
+            nest_u(s, i)
+        nest_row(s, before, 2, 1)
+
+        @pl.when(more)
+        def _():
+            for copy, cond in middle_copies(blk):
+                pl.when(cond)(copy.start)
 
         @pl.when(blk > 0)
         def _():
@@ -331,31 +340,36 @@
             arrived(n_p.at[s - 1, 6], nm_recv.at[blk - 1, 1], ~last)
             nest_u(s - 1, 0)
             nest_u(s - 1, 5)
-        pl.when(blk < 2)(lambda: take_ghosts(blk))
-
+        for i in range(2):
+            arrived(n_p.at[s, i], nx_recv.at[blk, 0, i], ~first)
+            arrived(n_p.at[s, 5 + i], nx_recv.at[blk, 1, i], ~last)
+
+        @pl.when(blk == 0)
+        def _():
+            for i in range(3):
+                arrived(to_up[i + 2][1], ni_recv.at[0, i], ~first)
+                arrived(to_down[i + 2][1], ni_recv.at[1, i], ~last)
         above_nest(s, before)
-        for i in range(6):
+        for i in (0, 1, 4, 5):
             nest_u(s, i)
         below_nest(before)
-        for i in (2, 1, 3, 4, 0):
-            nest_row(s, before, i, (i + 2) // RATIO)
-
-        @pl.when(blk < BLOCKS - 1)
-        def _():
-            for copy, cond in middle_copies(blk):
-                pl.when(cond)(copy.start)
-
-        above_nest(s + 1, after)
-        for i in range(1, 5):
+        nest_row(s, before, 3, 1)
+        nest_row(s, before, 1, 1)
+        pl.when(blk == 1)(lambda: take_ghosts(1))
+
+        for i in (2, 3):
             nest_u(s + 1, i)
-        below_nest(after)
-        up, down = end_copies(blk)
-        more = blk < BLOCKS - 1
         nest_row(s + 1, after, 2, 1)
         pl.when(more & ~last)(up[0].start)
         pl.when(more & ~first)(down[1].start)
+        nest_row(s, before, 4, 2)
+        above_nest(s + 1, after)
+        nest_u(s + 1, 4)
         nest_row(s + 1, after, 3, 1)
         pl.when(more & ~last)(up[1].start)
+        nest_row(s, before, 0, 0)
+        nest_u(s + 1, 1)
+        below_nest(after)
         nest_row(s + 1, after, 1, 1)
         pl.when(more & ~first)(down[0].start)
 
@@ -435,6 +449,12 @@
 
         @pl.when(it == 0)
         def _():
+            for copy, cond in parent_copies(0, p_in.at[0]):
+                pl.when(cond)(copy.start)
+            pl.when(~last)(parent_u_copy().start)
+
+        @pl.when(it == 0)
+        def _():
             fold[...] = jnp.where((spot >= 0) & (spot < RATIO), 1.0, 0.0).astype(BF16)
             block = lax.broadcasted_iota(jnp.int32, (levels, 3 * levels), 1)
             copies = (block % levels == lax.broadcasted_iota(jnp.int32, (levels, 3 * levels), 0)).astype(F32)
@@ -443,27 +463,25 @@
             mix[...] = jnp.where(block >= 2 * levels, m2, m1).astype(BF16)
             for name in ("np", "nu", "nv", "nk", "pk"):
                 loads[name].wait()
-            for i in range(3):
-                arrived(to_up[i + 2][1], ni_recv.at[0, i], ~first)
-                arrived(to_down[i + 2][1], ni_recv.at[1, i], ~last)
-            arrived(p_u.at[0], px_recv.at[0, 2], ~first)
         nest_block(it)
-        pl.when(it > 0)(lambda: start_feedback(it - 1))
 
         @pl.when(it == 2)
         def _():
             take_feedback(0, p_p.at[1, pl.ds(1, 3)])
             for copy, cond in parent_copies(1, p_p.at[1, pl.ds(1, 3)]):
                 pl.when(cond)(copy.start)
+        pl.when(it > 0)(lambda: start_feedback(it - 1))
+
+        @pl.when(it == 2)
+        def _():
             for copy in stores()[:3]:
                 copy.start()
+        pl.when(it == 0)(lambda: arrived(p_u.at[0], px_recv.at[0, 2], ~first))
         pl.when(it != 1)(lambda: parent_substep(it // 2))
     loop(0, BLOCKS, turn)
     outs = stores()
     for copy in outs[3:]:
         copy.start()
-    take_feedback(1, p_out.at[0])
-
     for o in range(OUTER):
         end_ghosts(o)
         for i in range(backs_to):
@@ -479,8 +497,10 @@
     for s, rows in ((0, p_in.at[0]), (1, p_p.at[1, pl.ds(1, 3)])):
         for copy, cond in parent_copies(s, rows):
             pl.when(cond)(copy.wait_send)
+    pl.when(~last)(parent_u_copy().wait_send)
     for wait in finish:
         wait()
+    take_feedback(1, p_out.at[0])
     for copy in outs:
         copy.wait()
 

time: 51 us -> 48.1 us (0.943)
  Pallas kernels: 48.7 us -> 45.8 us
    pallas_call x1, Pallas kernels: 47.5 us -> 44.5 us  [per_device(): call(lead)(*args)]
where the time goes in v4:
time: 48.1 us; the launch traced here: 47.9 us
  Pallas kernels  45.8 us (95%)
  between operations  1.55 us (3%)
  loops' own time  0.61 us (1%)
    pallas_call x1, Pallas kernels, per_device(): call(lead)(*args)  44.5 us
    pallas_call x1, Pallas kernels, per_device(): pl.pallas_call(put_out, out_shape=[jax.ShapeDtypeStruct((2, rows) + row,...  1.23 us

profile of v4, /device:TPU:8, one launch (start us, length us, event | category | flops | bytes accessed | tf_op | source)
XLA Modules:
  0.0 47.9 jit_solution(11164320432860094410)
XLA Ops:
  1.3 45.1 %conditional.1 = ((f32[2,3,32,768]{3,2,1,0:T(8,128)S(1)}, f32[2,3,32,768]{3,2,1,0:T(8,128)S(1)}, f32[2,3,32,768]{3,2,1,0:T(8,128)S(1)})) conditional(s32[]{:T(128)} %clamp.3, (s32[60]{0:T(128)}, s32[511]{0:T(512)}, f32[32,32]{1,0:T(8,128)}, f32[2,3,32,768]{3,2,1,0:T(8,128)}, f32[2,3,32,768]{3,2,1,0:T(8,128)}, ...), branch_computations={%region_0.1_spmd, %region_1.2_spmd, %region_2.3_spmd, %region_3.4_... | conditional | flops 300000000 | bytes 4200008 | solution.py:554
  1.3 44.5 %branch_1_fun.1 = (f32[2,3,32,768]{3,2,1,0:T(8,128)S(1)}, f32[2,3,32,768]{3,2,1,0:T(8,128)S(1)}, f32[2,3,32,768]{3,2,1,0:T(8,128)S(1)}) custom-call(s32[60]{0:T(128)} %get-tuple-element.147.row0_in, s32[511]{0:T(512)} %get-tuple-element.148.col0_in, f32[32,32]{1,0:T(8,128)} %get-tuple-element.149.vert_in, f32[2,3,32,768]{3,2,1,0:T(8,128)} %get-tuple-element.150.p_in, ...), custom_call_target="tpu_custom_call" | custom-call | flops 300000000 | bytes 4200000 | tf_op jit(solution)/shard_map/cond/branch_1_fun/pallas_call | solution.py:553
  46.5 1.2 %shard_map.94 = (f32[2,3,32,768]{3,2,1,0:T(8,128)}, f32[2,3,32,768]{3,2,1,0:T(8,128)}, f32[2,3,32,768]{3,2,1,0:T(8,128)}) custom-call(f32[2,3,32,768]{3,2,1,0:T(8,128)S(1)} %get-tuple-element.219.p, f32[2,3,32,768]{3,2,1,0:T(8,128)S(1)} %get-tuple-element.220.u, f32[2,3,32,768]{3,2,1,0:T(8,128)S(1)} %get-tuple-element.221.v), custom_call_target="tpu_custom_call" | custom-call | tf_op jit(solution)/shard_map/pallas_call | solution.py:555
